TPU v7x, 32 devices: a whole 2x2x4 slice. The times are simulated.
32 devices in a mesh: req: 8 (over z, y), mlp: 4 (over x, core).
Axes of the slice: x: 2, y: 2, z: 4, core: 2. Of those that a mesh axis runs over, the one named last changes fastest.
Arguments:
- tokens: bfloat16 [8192, 1536], P(('req', 'mlp')), may hold values from -6 to 6
- attn_gain: float32 [1536], replicated, may hold values from 0.1 to 1.9
- w_query: bfloat16 [1536, 1536], replicated, may hold values from -0.15625 to 0.15625
- w_keyval: bfloat16 [1536, 256], replicated, may hold values from -0.15625 to 0.15625
- w_out: bfloat16 [1536, 1536], replicated, may hold values from -0.15625 to 0.15625
- ffn_gain: float32 [1536], replicated, may hold values from 0.1 to 1.9
- w_gate: bfloat16 [1536, 4608], P('req', 'mlp'), may hold values from -0.15625 to 0.15625
- w_up: bfloat16 [1536, 4608], P('req', 'mlp'), may hold values from -0.15625 to 0.15625
- w_down: bfloat16 [1536, 4608], P('req', 'mlp'), may hold values from -0.09375 to 0.09375
- prefix_kv: bfloat16 [2, 64, 512, 256], P(None, 'req'), may hold values from -60 to 60, as said below
- own_prefix: bfloat16 [8, 512, 256], P('req'), may hold values from -60 to 60, as said below
- leaf_parent: int32 [8], replicated, may hold values from 0 to 63
- node_parent: int32 [64], replicated, may hold values from 0 to 63
- seg_lengths: int32 [3, 64], replicated, may hold values from 1 to 512
Outputs:
- layer_out: bfloat16 [8192, 1536], P(('req', 'mlp'))
Inputs may be any that keep to these rules, and one draw needn't show every extreme that they name: `prefix_kv`: columns below 128 are keys, the rest values. `own_prefix`: columns below 128 are keys, the rest values.
All inputs are finite; a program needn't handle non-finite values.
Results may differ from a plain program's by a relative error of at most 0.018.
Values may be sent and summed in bfloat16 or wider, within the bound.
A program may use at most 192 MiB of HBM per device.

v0:
```python
import jax
import jax.numpy as jnp
from jax import lax
from jax.sharding import PartitionSpec as P

HEADS = 12
HD = 128
WINDOW = 1024


EPS = 1e-06


def rms_scale(values, gain):
    wide = values.astype(jnp.float32)
    return wide * lax.rsqrt(jnp.mean(wide * wide, axis=-1, keepdims=True) + EPS) * gain


def rotate(values, where_at):
    half_dim = values.shape[-1] // 2
    freqs = 10000.0 ** (-jnp.arange(half_dim, dtype=jnp.float32) / half_dim)
    angles = where_at.astype(jnp.float32)[:, None] * freqs[None, :]
    cosine = jnp.cos(angles)[:, None, :]
    sine = jnp.sin(angles)[:, None, :]
    first = values[..., :half_dim]
    second = values[..., half_dim:]
    return jnp.concatenate([first * cosine - second * sine, first * sine + second * cosine], -1)


def attend(queries, piece, key_at, key_live, query_at):
    scores = jnp.einsum("thd,kd->thk", queries, piece[:, :HD], preferred_element_type=jnp.float32)
    spacing = query_at[:, None] - key_at[None, :]
    allowed = (key_live[None, :] & (spacing >= 0) & (spacing < WINDOW))[:, None, :]
    top = jnp.max(jnp.where(allowed, scores, -jnp.inf), axis=-1)
    safe_top = jnp.where(jnp.isfinite(top), top, 0.0)
    weights = jnp.where(allowed, jnp.exp(scores - safe_top[..., None]), 0.0)
    mixed = jnp.einsum(
        "thk,kd->thd",
        weights.astype(jnp.bfloat16),
        piece[:, HD:],
        preferred_element_type=jnp.float32,
    )
    return (top, jnp.sum(weights, axis=-1), mixed)


def combine(first, second):
    top = jnp.maximum(first[0], second[0])
    safe_top = jnp.where(jnp.isfinite(top), top, 0.0)
    scale_first = jnp.exp(first[0] - safe_top)
    scale_second = jnp.exp(second[0] - safe_top)
    denom = first[1] * scale_first + second[1] * scale_second
    mixed = first[2] * scale_first[..., None] + second[2] * scale_second[..., None]
    return (top, denom, mixed)


def body(
    tokens,
    attn_gain,
    w_query,
    w_keyval,
    w_out,
    ffn_gain,
    w_gate,
    w_up,
    w_down,
    prefix_kv,
    own_prefix,
    leaf_parent,
    node_parent,
    seg_lengths,
):
    tok_rows = tokens.shape[0]
    requests = lax.axis_size("req")
    mine = lax.axis_index("req")
    position_group = lax.axis_index("mlp")
    node_dev = prefix_kv.shape[1]
    seg_slot = prefix_kv.shape[2]
    leaf = leaf_parent[mine]
    upper = node_parent[leaf]
    len_zero = seg_lengths[0, upper]
    len_one = seg_lengths[1, leaf]
    len_two = seg_lengths[2, mine]
    total = len_zero + len_one + len_two
    query_at = total + position_group * tok_rows + jnp.arange(tok_rows, dtype=jnp.int32)
    normed = rms_scale(tokens, attn_gain).astype(jnp.bfloat16)
    query_full = jnp.dot(normed, w_query, preferred_element_type=jnp.float32).reshape(
        tok_rows, HEADS, HD
    )
    queries = (rotate(query_full, query_at) * HD ** (-0.5)).astype(jnp.bfloat16)
    keyval_full = jnp.dot(normed, w_keyval, preferred_element_type=jnp.float32)
    new_keys = rotate(keyval_full[:, None, :HD], query_at)[:, 0].astype(jnp.bfloat16)
    new_vals = keyval_full[:, HD:].astype(jnp.bfloat16)
    new_keyval = jnp.concatenate([new_keys, new_vals], 1)
    start_state = (
        jnp.full((tok_rows, HEADS), -jnp.inf, jnp.float32),
        jnp.zeros((tok_rows, HEADS), jnp.float32),
        jnp.zeros((tok_rows, HEADS, HD), jnp.float32),
    )
    piece = lax.all_gather(new_keyval, "mlp", axis=0, tiled=True)
    piece_at = total + jnp.arange(piece.shape[0], dtype=jnp.int32)
    live = jnp.ones((piece.shape[0],), dtype=bool)
    own_state = combine(start_state, attend(queries, piece, piece_at, live, query_at))
    level_zero = node_parent[leaf_parent]
    wanted = jnp.stack([level_zero, leaf_parent], 1)
    owned = wanted // node_dev == mine
    local_slot = wanted % node_dev
    picker = (
        (local_slot[:, :, None] == jnp.arange(node_dev, dtype=jnp.int32)[None, None, :])
        & owned[:, :, None]
    ).astype(jnp.bfloat16)
    owners = wanted[mine] // node_dev
    from_owner = (jnp.arange(requests, dtype=jnp.int32)[:, None] == owners[None, :]).astype(
        jnp.bfloat16
    )
    outgoing = jnp.einsum(
        "rln,lnsc->rlsc", picker, prefix_kv, preferred_element_type=jnp.float32
    ).astype(jnp.bfloat16)
    arrived = lax.all_to_all(outgoing, "req", split_axis=0, concat_axis=0, tiled=True)
    levels = jnp.einsum(
        "rl,rlsc->lsc", from_owner, arrived, preferred_element_type=jnp.float32
    ).astype(jnp.bfloat16)
    offsets = jnp.arange(seg_slot, dtype=jnp.int32)
    cached = jnp.concatenate([levels[0], levels[1], own_prefix[0]], 0)
    cached_at = jnp.concatenate([offsets, len_zero + offsets, len_zero + len_one + offsets], 0)
    cached_live = jnp.concatenate([offsets < len_zero, offsets < len_one, offsets < len_two], 0)
    merged = combine(own_state, attend(queries, cached, cached_at, cached_live, query_at))
    context = (merged[2] / merged[1][..., None]).reshape(tok_rows, HEADS * HD).astype(jnp.bfloat16)
    attn_out = jnp.dot(context, w_out, preferred_element_type=jnp.float32)
    resid = (tokens.astype(jnp.float32) + attn_out).astype(jnp.bfloat16)
    ffn_in = rms_scale(resid, ffn_gain).astype(jnp.bfloat16)
    all_rows = lax.all_gather(ffn_in, "mlp", axis=0, tiled=True)
    gate_full, up_full, down_full = (
        lax.all_gather(w_gate, "req", axis=0, tiled=True),
        lax.all_gather(w_up, "req", axis=0, tiled=True),
        lax.all_gather(w_down, "req", axis=0, tiled=True),
    )
    gate = jnp.dot(all_rows, gate_full, preferred_element_type=jnp.float32)
    upward = jnp.dot(all_rows, up_full, preferred_element_type=jnp.float32)
    hidden = (jax.nn.gelu(gate, approximate=True) * upward).astype(jnp.bfloat16)
    summed = lax.psum_scatter(
        lax.dot_general(
            hidden, down_full, (((1,), (1,)), ((), ())), preferred_element_type=jnp.float32
        ).astype(jnp.bfloat16),
        "mlp",
        scatter_dimension=0,
        tiled=True,
    ).astype(jnp.float32)
    return (resid.astype(jnp.float32) + summed).astype(jnp.bfloat16)


def solution(mesh):
    return jax.shard_map(
        body,
        mesh=mesh,
        in_specs=(
            P(("req", "mlp"), None),
            P(),
            P(),
            P(),
            P(),
            P(),
            P("req", "mlp"),
            P("req", "mlp"),
            P("req", "mlp"),
            P(None, "req", None, None),
            P("req", None, None),
            P(),
            P(),
            P(),
        ),
        out_specs=P(("req", "mlp"), None),
        check_vma=False,
    )
```

profile of v0, /device:TPU:0, one launch (start us, length us, event | category | flops | bytes accessed | tf_op | source)
XLA Modules:
  0.0 413.9 jit_solution(11993457885792332962)
XLA Ops:
  6.5 0.7 all-gather.7.cloned.1.call-update
  7.3 0.7 compare_select_fusion
  7.9 1.3 gather_fusion
  9.2 0.7 and_select_fusion.1
  9.9 0.7 fusion.58
  10.6 4.7 %convert_bitcast_fusion = bf16[8,2,512,256]{3,0,2,1:T(8,128)(2,1)S(1)} fusion(bf16[2,8,512,256]{3,2,1,0:T(8,128)(2,1)} %param.23, s32[8,2]{0,1:T(2,128)S(1)} %get-tuple-element.24, pred[8,2]{0,1:T(4,128)(4,1)S(1)} %fusion.58), kind=kOutput, calls=%fused_computation.28 | convolution fusion | flops 35651840 | bytes 8388688 | tf_op jit(solution)/shard_map/rln,lnsc->rlsc/dot_general | solution.py:115
  15.3 2.9 copy.33
  18.2 7.4 %all-to-all-start = ((bf16[8,2,512,256]{3,2,1,0:T(8,128)(2,1)}), bf16[8,2,512,256]{3,2,1,0:T(8,128)(2,1)}, u32[]{:S(2)}, u32[]{:S(2)}) async-start(bf16[8,2,512,256]{3,2,1,0:T(8,128)(2,1)} %copy.33), calls=%async_computation | async-start | bytes 8388608 | tf_op jit(solution)/shard_map/all_to_all | solution.py:118
  31.3 4.4 %fusion.41 = f32[256,1536]{0,1:T(8,128)S(1)} fusion(bf16[1536,1536]{1,0:T(8,128)(2,1)} %param.16, bf16[256,1536]{1,0:T(8,128)(2,1)S(1)} %copy-done.3, f32[1536]{0:T(1024)S(1)} %copy-done.9, f32[256]{0:T(256)S(1)} %add_rsqrt_fusion.1), kind=kOutput, calls=%fused_computation.65 | convolution fusion | flops 1209532416 | bytes 7085056 | tf_op jit(solution)/shard_map/dot_general | solution.py:86
  36.3 1.7 copy.45
  38.7 0.6 constant_dynamic-slice_fusion
  41.7 1.3 iota_compare_fusion.2
  44.6 1.9 multiply_subtract_fusion
  46.9 7.2 %all_gather.15 = bf16[1024,256]{0,1:T(8,128)(2,1)S(1)} all-gather(bf16[256,256]{0,1:T(8,128)(2,1)S(1)} %pad_maximum_fusion.1), channel_id=1, replica_groups=mesh['req'=8,'mlp'=4] {'mlp'}, dimensions={0}, use_global_device_ids=true | all-gather | bytes 655360 | tf_op jit(solution)/shard_map/all_gather | solution.py:99
  54.4 1.9 select_reduce_fusion.1
  56.3 3.9 fusion.2
  60.2 3.8 fusion.7
  64.6 92.6 %all-to-all-done = bf16[8,2,512,256]{3,2,1,0:T(8,128)(2,1)} async-done(((bf16[8,2,512,256]{3,2,1,0:T(8,128)(2,1)}), bf16[8,2,512,256]{3,2,1,0:T(8,128)(2,1)}, u32[]{:S(2)}, u32[]{:S(2)}) %all-to-all-start) | async-done | bytes 4194336 | tf_op jit(solution)/shard_map/all_to_all | solution.py:118
  157.1 4.9 %fusion.19 = bf16[2,1,512,256]{3,1,2,0:T(2,128)(2,1)S(1)} fusion(pred[8,2,1,1]{0,2,3,1:T(4,128)(4,1)S(1)} %copy.38, bf16[8,2,512,256]{3,2,1,0:T(8,128)(2,1)} %all-to-all-done), kind=kOutput, calls=%fused_computation.24 | convolution fusion | flops 4194304 | bytes 4718608 | tf_op jit(solution)/shard_map/rl,rlsc->lsc/dot_general | solution.py:119
  162.3 8.0 %select_reduce_fusion = (f32[256,12]{0,1:T(8,128)S(1)}, f32[256,12,1536]{2,0,1:T(8,128)}) fusion(pred[256,1536]{1,0:T(8,128)(4,1)S(1)} %fusion.33, bf16[256,12,128]{2,0,1:T(8,128)(2,1)S(1)} %fusion.31, bf16[1536,256]{1,0:T(8,128)(2,1)S(1)} %pad_maximum_fusion), kind=kOutput, calls=%fused_computation.2 | convolution fusion | flops 1217393664 | bytes 20459520 | tf_op jit(solution)/shard_map/thd,kd->thk/dot_general | solution.py:31
  170.3 10.5 %fusion = f32[256,12]{0,1:T(8,128)S(1)} fusion(f32[256,12,1536]{2,0,1:T(8,128)} %get-tuple-element.29, f32[256,12]{0,1:T(8,128)S(1)} %is-finite_select_fusion, pred[256,1536]{1,0:T(8,128)(4,1)S(1)} %fusion.33), kind=kLoop, calls=%fused_computation.3 | loop fusion | flops 14152704 | bytes 19292160 | tf_op jit(solution)/shard_map/reduce_sum | solution.py:43
  180.8 9.0 %divide_convert_fusion = bf16[256,12,128]{0,2,1:T(8,128)(2,1)S(1)} fusion(f32[256,12,128]{0,2,1:T(8,128)} %fusion.7, f32[256,12,1536]{2,0,1:T(8,128)} %get-tuple-element.29, f32[256,12]{0,1:T(8,128)S(1)} %is-finite_select_fusion, pred[256,1536]{1,0:T(8,128)(4,1)S(1)} %fusion.33, f32[256,12]{0,1:T(8,128)S(1)} %get-tuple-element.5, ...), kind=kOutput, calls=%fused_computation.46 | convolution fusion | flops 1224867840 | bytes 22118400 | tf_op jit(solution)/shard_map/thk,kd->thd/dot_general | solution.py:37
  189.8 1.5 multiply_reduce_fusion
  191.4 1.1 multiply_convert_fusion
  192.5 0.7 all-gather.9.cloned.1.call-update
  193.9 26.0 %all-gather.5.cloned.1.call-done = bf16[1024,1536]{1,0:T(8,128)(2,1)} async-done(((bf16[256,1536]{1,0:T(8,128)(2,1)}), bf16[1024,1536]{1,0:T(8,128)(2,1)}) %all-gather.5.cloned.1.call-update) | async-done | bytes 3145744 | tf_op jit(solution)/shard_map/all_gather | solution.py:131
  219.9 9.3 %fusion.67 = f32[1024,1152]{1,0:T(8,128)} fusion(bf16[1024,1536]{1,0:T(8,128)(2,1)} %all-gather.5.cloned.1.call-done, bf16[1536,1152]{1,0:T(8,128)(2,1)} %all-gather.7.cloned.1.call-done), kind=kOutput, calls=%fused_computation.136 | convolution fusion | flops 3623878656 | bytes 11403264 | tf_op jit(solution)/shard_map/dot_general | solution.py:137
  229.2 58.1 %all-gather.9.cloned.1.call-done = bf16[1536,1152]{1,0:T(8,128)(2,1)} async-done(((bf16[192,1152]{1,0:T(8,128)(2,1)}), bf16[1536,1152]{1,0:T(8,128)(2,1)}) %all-gather.9.cloned.1.call-update) | async-done | bytes 3538960 | tf_op jit(solution)/shard_map/all_gather | solution.py:134
  287.3 65.7 %all-gather.11.cloned.1.call-done = bf16[1536,1152]{1,0:T(8,128)(2,1)} async-done(((bf16[192,1152]{1,0:T(8,128)(2,1)}), bf16[1536,1152]{1,0:T(8,128)(2,1)}) %all-gather.11.cloned.1.call-update) | async-done | bytes 3538960 | tf_op jit(solution)/shard_map/all_gather | solution.py:135
  353.1 15.5 %convolution_convert_fusion = bf16[1024,1536]{1,0:T(8,128)(2,1)} fusion(bf16[1536,1152]{1,0:T(8,128)(2,1)} %all-gather.11.cloned.1.call-done, bf16[1024,1536]{1,0:T(8,128)(2,1)} %all-gather.5.cloned.1.call-done, bf16[1536,1152]{1,0:T(8,128)(2,1)} %all-gather.9.cloned.1.call-done, f32[1024,1152]{1,0:T(8,128)} %fusion.67), kind=kOutput, calls=%fused_computation.30 | convolution fusion | flops 7261126656 | bytes 18087936 | tf_op jit(solution)/shard_map/dot_general | solution.py:141
  368.6 36.6 %reduce-scatter.2.cloned.1.call-done = bf16[256,1536]{1,0:T(8,128)(2,1)} async-done(((bf16[1024,1536]{1,0:T(8,128)(2,1)}), bf16[256,1536]{1,0:T(8,128)(2,1)}) %reduce-scatter.2.cloned.1.call-update) | async-done | bytes 786448 | tf_op jit(solution)/shard_map/reduce_scatter | solution.py:140
  405.2 2.2 add_convert_fusion
  (70 shorter events, 7.3 us)
Async XLA Ops:
  6.5 24.2 %copy-start = (bf16[1536,256]{1,0:T(8,128)(2,1)S(1)}, bf16[1536,256]{1,0:T(8,128)(2,1)}, u32[]{:S(2)}) copy-start(bf16[1536,256]{1,0:T(8,128)(2,1)} %param.17) | copy-start | bytes 2359300
  6.5 187.3 %all-gather.7.cloned.1.call-start = ((), (), s32[]{:S(2)}) async-start(), calls=%async_computation.3 | async-start | bytes 3981312 | tf_op jit(solution)/shard_map/all_gather | solution.py:133
  18.2 7.7 %copy-start.7 = (s32[8]{0:T(128)S(1)}, s32[8]{0:T(128)}, u32[]{:S(2)}) copy-start(s32[8]{0:T(128)} %param.25) | copy-start | bytes 100
  18.2 10.2 %copy-start.2 = (s32[64]{0:T(128)S(1)}, s32[64]{0:T(128)}, u32[]{:S(2)}) copy-start(s32[64]{0:T(128)} %param.26) | copy-start | bytes 772
  18.2 12.2 %copy-start.3 = (bf16[256,1536]{1,0:T(8,128)(2,1)S(1)}, bf16[256,1536]{1,0:T(8,128)(2,1)}, u32[]{:S(2)}) copy-start(bf16[256,1536]{1,0:T(8,128)(2,1)} %param.14) | copy-start | bytes 2359300
  18.2 12.5 %copy-start.9 = (f32[1536]{0:T(1024)S(1)}, f32[1536]{0:T(1024)}, u32[]{:S(2)}) copy-start(f32[1536]{0:T(1024)} %param.15) | copy-start | bytes 18436
  18.2 138.9 %all-to-all-start = ((bf16[8,2,512,256]{3,2,1,0:T(8,128)(2,1)}), bf16[8,2,512,256]{3,2,1,0:T(8,128)(2,1)}, u32[]{:S(2)}, u32[]{:S(2)}) async-start(bf16[8,2,512,256]{3,2,1,0:T(8,128)(2,1)} %copy.33), calls=%async_computation | async-start | bytes 8388608 | tf_op jit(solution)/shard_map/all_to_all | solution.py:118
  25.6 194.3 %all-gather.5.cloned.1.call-start = ((), (), s32[]{:S(2)}) async-start(), calls=%async_computation.2 | async-start | bytes 3932160 | tf_op jit(solution)/shard_map/all_gather | solution.py:131
  35.7 3.0 copy-start.8
  64.6 97.7 %copy-start.5 = (bf16[1,512,256]{2,1,0:T(8,128)(2,1)S(1)}, bf16[1,512,256]{2,1,0:T(8,128)(2,1)}, u32[]{:S(2)}) copy-start(bf16[1,512,256]{2,1,0:T(8,128)(2,1)} %param.24) | copy-start | bytes 786436
  170.3 19.5 %slice-start = ((s8[4718592]{0:T(1024)(128)(4,1)}), s8[524288]{0:T(1024)(128)(4,1)S(1)}, s32[]{:S(2)}) async-start(s8[4718592]{0:T(1024)(128)(4,1)} %bitcast.58), calls=%async_computation.7 | async-start | bytes 1048576
  180.8 9.0 %slice-start.1 = ((s8[4718592]{0:T(1024)(128)(4,1)}), s8[4194304]{0:T(1024)(128)(4,1)S(1)}, s32[]{:S(2)}) async-start(s8[4718592]{0:T(1024)(128)(4,1)} %bitcast.58), calls=%async_computation.8 | async-start | bytes 8388608
  180.8 9.0 %copy-start.4 = (bf16[256,1536]{1,0:T(8,128)(2,1)S(1)}, bf16[256,1536]{1,0:T(8,128)(2,1)}, u32[]{:S(2)}) copy-start(bf16[256,1536]{1,0:T(8,128)(2,1)} %param.14) | copy-start | bytes 2359300
  189.8 1.5 copy-start.6
  192.5 94.8 %all-gather.9.cloned.1.call-start = ((), (), s32[]{:S(2)}) async-start(), calls=%async_computation.4 | async-start | bytes 3981312 | tf_op jit(solution)/shard_map/all_gather | solution.py:134
  193.2 159.9 %all-gather.11.cloned.1.call-start = ((), (), s32[]{:S(2)}) async-start(), calls=%async_computation.5 | async-start | bytes 3981312 | tf_op jit(solution)/shard_map/all_gather | solution.py:135
  193.8 211.4 %reduce-scatter.2.cloned.1.call-start = ((), (), s32[]{:S(2)}) async-start(), calls=%async_computation.6 | async-start | bytes 3932160 | tf_op jit(solution)/shard_map/reduce_scatter | solution.py:140
  353.1 54.3 %copy-start.1 = (bf16[1536,256]{1,0:T(8,128)(2,1)S(1)}, bf16[1536,256]{1,0:T(8,128)(2,1)}, u32[]{:S(2)}) copy-start(bf16[1536,256]{1,0:T(8,128)(2,1)} %param.17) | copy-start | bytes 2359300
Sparse Core Ops, SparseCore 0:
  9.5 140.4 all-gather.6
  192.6 27.2 all-gather.4
  222.1 65.1 all-gather.8
  289.3 63.6 all-gather.10
  368.7 36.4 reduce-scatter.1
where the time goes:
time: 414 us
  waiting for transfers between devices  281 us (68%)
  matrix products  63.6 us (15%)
  other arithmetic  26.7 us (6%)
  between operations  19.3 us (5%)
  local copies, waits for them, and re-layouts  8.59 us (2%)
  starting transfers between devices  7.58 us (2%)
  blocking collectives  7.17 us (2%)
    all_to_all x1, waiting for transfers between devices, body(): lax.all_to_all(outgoing, 'req', split_axis=0, concat_axis=0, tiled=True)  92.6 us
    all_gather x1, waiting for transfers between devices, body(): lax.all_gather(w_down, 'req', axis=0, tiled=True)  65.7 us
    all_gather x1, waiting for transfers between devices, body(): lax.all_gather(w_up, 'req', axis=0, tiled=True)  58.1 us
    reduce_scatter x1, waiting for transfers between devices, body(): lax.psum_scatter(lax.dot_general(hidden, down_full, (((1,), (1,)), ((), (...  36.6 us
    all_gather x1, waiting for transfers between devices, body(): all_rows = lax.all_gather(ffn_in, 'mlp', axis=0, tiled=True)  26 us
    dot_general x1, matrix products, body(): lax.dot_general(hidden, down_full, (((1,), (1,)), ((), ())), preferred_el...  15.5 us
    reduce_sum x2, other arithmetic, attend(): return (top, jnp.sum(weights, axis=-1), mixed)  14.4 us
    dot_general x2, matrix products, attend(): jnp.einsum('thk,kd->thd', weights.astype(jnp.bfloat16), piece[:, HD:], pr...  12.7 us
  transfers between devices with their start and end apart: 6, of which 5 were waited for; matrix products, arithmetic and copies ran while one was open for 20% of the time, Pallas kernels for 0%

commit v1 on v0

v1 whole, which is shorter than its diff:
```python
import functools

import jax
import jax.numpy as jnp
from jax import lax
from jax.experimental import pallas as pl
from jax.experimental.pallas import tpu as pltpu
from jax.sharding import PartitionSpec as P

HEADS = 12
HD = 128
WINDOW = 1024


EPS = 1e-06


def rms_scale(values, gain):
    wide = values.astype(jnp.float32)
    return wide * lax.rsqrt(jnp.mean(wide * wide, axis=-1, keepdims=True) + EPS) * gain


def rotate(values, where_at):
    half_dim = values.shape[-1] // 2
    freqs = 10000.0 ** (-jnp.arange(half_dim, dtype=jnp.float32) / half_dim)
    angles = where_at.astype(jnp.float32)[:, None] * freqs[None, :]
    cosine = jnp.cos(angles)[:, None, :]
    sine = jnp.sin(angles)[:, None, :]
    first = values[..., :half_dim]
    second = values[..., half_dim:]
    return jnp.concatenate([first * cosine - second * sine, first * sine + second * cosine], -1)


LINE = 4
MASKED = -1e30


def layer_kernel(
    dims, q_ref, kv_ref, ok_ref, tok_ref, gain_ref, wout_hbm, wg_hbm, wu_hbm, wd_hbm, out_ref,
    w_all, w_out, bias, ctx, rows_all, hidden, part, landed,
    load_sem, zs, zr, ys, yr, ts, tr, ps, pr,
):
    n_req, n_mlp = dims
    cross = n_req // LINE
    me, mine = lax.axis_index("req"), lax.axis_index("mlp")
    za, yb = me // cross, me % cross
    depth = wg_hbm.shape[0]
    tok = tok_ref.shape[0]
    model = tok_ref.shape[1]
    chunk = model // LINE
    keys = kv_ref.shape[0]

    loads = [
        pltpu.make_async_copy(ref, w_all.at[w, pl.ds(pl.multiple_of(me * depth, 16), depth)], load_sem.at[w])
        for w, ref in enumerate((wg_hbm, wu_hbm, wd_hbm))
    ]
    loads.append(pltpu.make_async_copy(wout_hbm, w_out, load_sem.at[3]))
    for load in loads:
        load.start()

    barrier = pltpu.get_barrier_semaphore()
    for k in range(1, LINE):
        pl.semaphore_signal(barrier, inc=1, device_id={"req": ((za + k) % LINE) * cross + yb})
    for k in range(1, cross):
        pl.semaphore_signal(barrier, inc=1, device_id={"req": za * cross + (yb + k) % cross})
    for k in range(1, n_mlp):
        pl.semaphore_signal(barrier, inc=1, device_id={"mlp": (mine + k) % n_mlp})
    pl.semaphore_wait(barrier, LINE + cross + n_mlp - 3)

    def block(w, a, b):
        return w_all.at[w, pl.ds(pl.multiple_of((a * cross + b) * depth, 16), depth)]

    def z_copy(w, a, toward, side):
        return pltpu.make_async_remote_copy(
            src_ref=block(w, a, yb), dst_ref=block(w, a, yb),
            send_sem=zs.at[w, a, side], recv_sem=zr.at[w, a],
            device_id={"req": toward * cross + yb},
        )

    def y_copy(w, a, b, toward, side):
        return pltpu.make_async_remote_copy(
            src_ref=block(w, a, b), dst_ref=block(w, a, b),
            send_sem=ys.at[w, a, b, side], recv_sem=yr.at[w, a, b],
            device_id={"req": za * cross + toward},
        )

    def y_send(w, a, b, steps, finish=False):
        for step in steps:
            @pl.when((yb + step >= 0) & (yb + step < cross))
            def _():
                copy = y_copy(w, a, b, yb + step, (step + 1) // 2)
                copy.wait_send() if finish else copy.start()

    def z_send(w, a, steps, finish=False):
        for step in steps:
            @pl.when((za + step >= 0) & (za + step < LINE))
            def _():
                copy = z_copy(w, a, za + step, (step + 1) // 2)
                copy.wait_send() if finish else copy.start()

    def own(w, finish=False):
        z_send(w, za, (-1, 1), finish)
        y_send(w, za, yb, (-1, 1), finish)

    def relay(w, dist, finish=False):
        for side in (-1, 1):
            origin = za + side * dist

            @pl.when((origin >= 0) & (origin < LINE))
            def _():
                if not finish:
                    z_copy(w, origin, za, 0).wait_recv()
                z_send(w, origin, (-side,), finish)
                y_send(w, origin, yb, (-1, 1), finish)

    def y_wait(w, a):
        for dist in range(1, cross):
            for side in (-1, 1):
                origin = yb + side * dist

                @pl.when((origin >= 0) & (origin < cross))
                def _():
                    y_copy(w, a, origin, yb, 0).wait_recv()
                    y_send(w, a, origin, (-side,))

    for load in loads[:3]:
        load.wait()
    own(0)
    own(1)

    query_row = lax.broadcasted_iota(jnp.int32, (tok, keys), 0)
    slot = lax.broadcasted_iota(jnp.int32, (tok, keys), 1)
    allowed = (slot > query_row) & (slot <= query_row + WINDOW) & (ok_ref[...] > 0)
    bias[...] = jnp.where(allowed, 0.0, MASKED)

    def heads(first, count):
        @pl.loop(first, first + count)
        def _(h):
            cols = pl.ds(pl.multiple_of(h * HD, HD), HD)
            scores = lax.dot_general(
                q_ref[:, cols], kv_ref[:, :HD], (((1,), (1,)), ((), ())),
                preferred_element_type=jnp.float32,
            ) + bias[...]
            weights = jnp.exp(scores - jnp.max(scores, axis=-1, keepdims=True))
            denom = jnp.sum(weights, axis=-1, keepdims=True)
            mixed = jnp.dot(
                weights.astype(jnp.bfloat16), kv_ref[:, HD:], preferred_element_type=jnp.float32
            )
            ctx[:, cols] = (mixed / denom).astype(jnp.bfloat16)

    third = HEADS // 3
    heads(0, third)
    relay(0, 1)
    heads(third, third)
    relay(1, 1)
    own(2)
    heads(2 * third, HEADS - 2 * third)
    relay(0, 2)
    loads[3].wait()

    @pl.loop(0, LINE)
    def _(c):
        cols = pl.ds(pl.multiple_of(c * chunk, 128), chunk)
        out_ref[:, cols] = (
            tok_ref[:, cols].astype(jnp.float32)
            + jnp.dot(ctx[...], w_out[:, cols], preferred_element_type=jnp.float32)
        ).astype(jnp.bfloat16)

    rows_all[mine] = rms_scale(out_ref[...], gain_ref[...]).astype(jnp.bfloat16)

    def t_copy(owner, toward):
        return pltpu.make_async_remote_copy(
            src_ref=rows_all.at[owner], dst_ref=rows_all.at[owner],
            send_sem=ts.at[toward], recv_sem=tr.at[owner], device_id={"mlp": toward},
        )

    others = [(mine + k) % n_mlp for k in range(1, n_mlp)]
    for toward in others:
        t_copy(mine, toward).start()
    relay(1, 2)
    relay(2, 1)
    relay(0, 3)
    relay(1, 3)
    relay(2, 2)
    for w in range(2):
        for a in range(LINE):
            y_wait(w, a)

    width = hidden.shape[2]
    tile = 384 if width % 384 == 0 else width

    def gate_up(g):
        for c in range(width // tile):
            cols = pl.ds(c * tile, tile)
            gate = jnp.dot(rows_all[g], w_all[0, :, cols], preferred_element_type=jnp.float32)
            upward = jnp.dot(rows_all[g], w_all[1, :, cols], preferred_element_type=jnp.float32)
            hidden[g, :, cols] = (jax.nn.gelu(gate, approximate=True) * upward).astype(jnp.bfloat16)

    @pl.loop(0, n_mlp)
    def _(k):
        g = (mine + k) % n_mlp

        @pl.when(k > 0)
        def _():
            t_copy(g, mine).wait_recv()

        gate_up(g)

    relay(2, 3)

    def p_copy(g, src, c):
        return pltpu.make_async_remote_copy(
            src_ref=part.at[g, c], dst_ref=landed.at[src, c],
            send_sem=ps.at[g, c], recv_sem=pr.at[src, c], device_id={"mlp": g},
        )

    def nth(k):
        second = jnp.where(za == 0, 1, za - 1)
        third_a = jnp.where(za == 3, 1, jnp.where(za == 2, 3, 2))
        fourth = jnp.where(za < 2, 3, 0)
        return jnp.where(k == 0, za, jnp.where(k == 1, second, jnp.where(k == 2, third_a, fourth)))

    @pl.loop(0, LINE)
    def _(k):
        a = nth(k)
        y_wait(2, a)

        @pl.loop(1, n_mlp + 1)
        def _(j):
            g = (mine + j) % n_mlp
            part[g, a] = lax.dot_general(
                hidden[g], w_all[2, pl.ds(pl.multiple_of(a * chunk, 16), chunk)],
                (((1,), (1,)), ((), ())), preferred_element_type=jnp.float32,
            ).astype(jnp.bfloat16)

            @pl.when(j < n_mlp)
            def _():
                p_copy(g, mine, a).start()

    @pl.loop(0, LINE)
    def _(k):
        a = nth(k)
        cols = pl.ds(pl.multiple_of(a * chunk, 128), chunk)
        total = part[mine, a].astype(jnp.float32)
        for g in others:
            p_copy(mine, g, a).wait_recv()
            total = total + landed[g, a].astype(jnp.float32)
        out_ref[:, cols] = (out_ref[:, cols].astype(jnp.float32) + total).astype(jnp.bfloat16)

    for toward in others:
        t_copy(mine, toward).wait_send()

    @pl.loop(0, LINE)
    def _(a):
        for g in others:
            p_copy(g, mine, a).wait_send()

    @pl.loop(0, 3)
    def _(w):
        own(w, True)
        for dist in range(1, LINE):
            relay(w, dist, True)

        @pl.loop(0, LINE)
        def _(a):
            for dist in range(1, cross):
                for side in (-1, 1):
                    origin = yb + side * dist

                    @pl.when((origin >= 0) & (origin < cross))
                    def _():
                        y_send(w, a, origin, (-side,), True)


def fused_layer(n_req, n_mlp, q, kv, ok, tokens, gain, w_out, w_gate, w_up, w_down):
    tok, model = tokens.shape
    depth, width = w_gate.shape
    chunk = model // LINE
    cross = n_req // LINE
    whole = pl.BlockSpec(memory_space=pltpu.VMEM)
    far = pl.BlockSpec(memory_space=pl.ANY)
    dma = pltpu.SemaphoreType.DMA
    half = jnp.bfloat16
    return pl.pallas_call(
        functools.partial(layer_kernel, (n_req, n_mlp)),
        out_shape=jax.ShapeDtypeStruct((tok, model), half),
        in_specs=[whole] * 5 + [far] * 4,
        out_specs=whole,
        scratch_shapes=[
            pltpu.VMEM((3, model, width), half),
            pltpu.VMEM(w_out.shape, half),
            pltpu.VMEM((tok, kv.shape[0]), jnp.float32),
            pltpu.VMEM((tok, HEADS * HD), half),
            pltpu.VMEM((n_mlp, tok, model), half),
            pltpu.VMEM((n_mlp, tok, width), half),
            pltpu.VMEM((n_mlp, LINE, tok, chunk), half),
            pltpu.VMEM((n_mlp, LINE, tok, chunk), half),
            dma((4,)),
            dma((3, LINE, 2)),
            dma((3, LINE)),
            dma((3, LINE, cross, 2)),
            dma((3, LINE, cross)),
            dma((n_mlp,)),
            dma((n_mlp,)),
            dma((n_mlp, LINE)),
            dma((n_mlp, LINE)),
        ],
        compiler_params=pltpu.CompilerParams(
            collective_id=0, has_side_effects=True, vmem_limit_bytes=58 * 1024 * 1024
        ),
    )(q, kv, ok, tokens, gain, w_out, w_gate, w_up, w_down)


def body(
    tokens, attn_gain, w_query, w_keyval, w_out, ffn_gain, w_gate, w_up, w_down,
    prefix_kv, own_prefix, leaf_parent, node_parent, seg_lengths,
):
    tok_rows = tokens.shape[0]
    requests = lax.axis_size("req")
    groups = lax.axis_size("mlp")
    mine = lax.axis_index("req")
    position_group = lax.axis_index("mlp")
    node_dev = prefix_kv.shape[1]
    seg_slot = prefix_kv.shape[2]
    leaf = leaf_parent[mine]
    upper = node_parent[leaf]
    len_zero = seg_lengths[0, upper]
    len_one = seg_lengths[1, leaf]
    len_two = seg_lengths[2, mine]
    total = len_zero + len_one + len_two

    share = seg_slot // groups
    level_zero = node_parent[leaf_parent]
    wanted = jnp.stack([level_zero, leaf_parent], 1)
    owned = wanted // node_dev == mine
    local_slot = wanted % node_dev
    picker = (
        (local_slot[:, :, None] == jnp.arange(node_dev, dtype=jnp.int32)[None, None, :])
        & owned[:, :, None]
    ).astype(jnp.bfloat16)
    owners = wanted[mine] // node_dev
    from_owner = (jnp.arange(requests, dtype=jnp.int32)[:, None] == owners[None, :]).astype(
        jnp.bfloat16
    )
    shared_rows = lax.dynamic_slice_in_dim(prefix_kv, position_group * share, share, 2)
    outgoing = jnp.einsum(
        "rln,lnsc->rlsc", picker, shared_rows, preferred_element_type=jnp.float32
    ).astype(jnp.bfloat16)
    arrived = lax.all_to_all(outgoing, "req", split_axis=0, concat_axis=0, tiled=True)

    query_at = total + position_group * tok_rows + jnp.arange(tok_rows, dtype=jnp.int32)
    normed = rms_scale(tokens, attn_gain).astype(jnp.bfloat16)
    keyval_full = jnp.dot(normed, w_keyval, preferred_element_type=jnp.float32)
    new_keys = rotate(keyval_full[:, None, :HD], query_at)[:, 0].astype(jnp.bfloat16)
    new_vals = keyval_full[:, HD:].astype(jnp.bfloat16)
    new_keyval = jnp.concatenate([new_keys, new_vals], 1)
    query_full = jnp.dot(normed, w_query, preferred_element_type=jnp.float32).reshape(
        tok_rows, HEADS, HD
    )
    queries = (rotate(query_full, query_at) * HD ** (-0.5)).astype(jnp.bfloat16)

    levels = jnp.einsum(
        "rl,rlsc->lsc", from_owner, arrived, preferred_element_type=jnp.float32
    ).astype(jnp.bfloat16)
    gathered = lax.all_gather(
        jnp.concatenate([levels[0], levels[1], new_keyval], 0), "mlp", axis=0
    )
    cached = gathered[:, : 2 * share].reshape(groups, 2, share, 2 * HD)
    laid = jnp.zeros((WINDOW + 3 * seg_slot + groups * tok_rows, 2 * HD), jnp.bfloat16)
    laid = lax.dynamic_update_slice(laid, cached[:, 0].reshape(seg_slot, 2 * HD), (WINDOW, 0))
    laid = lax.dynamic_update_slice(
        laid, cached[:, 1].reshape(seg_slot, 2 * HD), (WINDOW + len_zero, 0)
    )
    laid = lax.dynamic_update_slice(laid, own_prefix[0], (WINDOW + len_zero + len_one, 0))
    laid = lax.dynamic_update_slice(
        laid, gathered[:, 2 * share :].reshape(groups * tok_rows, 2 * HD), (WINDOW + total, 0)
    )
    first = total + position_group * tok_rows
    keys = WINDOW + tok_rows
    window = lax.dynamic_slice_in_dim(laid, first, keys, 0)
    used = (first - WINDOW + jnp.arange(keys, dtype=jnp.int32) >= 0).astype(jnp.int32)[None, :]
    return fused_layer(
        requests, groups, queries.reshape(tok_rows, HEADS * HD), window, used, tokens,
        ffn_gain[None, :], w_out, w_gate, w_up, w_down,
    )


def solution(mesh):
    return jax.shard_map(
        body,
        mesh=mesh,
        in_specs=(
            P(("req", "mlp"), None),
            P(),
            P(),
            P(),
            P(),
            P(),
            P("req", "mlp"),
            P("req", "mlp"),
            P("req", "mlp"),
            P(None, "req", None, None),
            P("req", None, None),
            P(),
            P(),
            P(),
        ),
        out_specs=P(("req", "mlp"), None),
        check_vma=False,
    )
```

time: 414 us -> 233 us (0.56)
  waiting for transfers between devices: 281 us -> 23.2 us
  Pallas kernels: 0 us -> 149 us
  matrix products: 63.6 us -> 5.69 us
  other arithmetic: 26.7 us -> 5.18 us
  local copies, waits for them, and re-layouts: 8.59 us -> 20 us
  blocking collectives: 7.17 us -> 0 us
    pallas_call x0 -> x1, Pallas kernels: none -> 149 us  [fused_layer(): pl.pallas_call(functools.partial(layer_kernel, (n_req, n_mlp)), out_shape...]
    all_gather x4 -> x1, waiting for transfers between devices: 150 us -> 6.54 us  [body(): lax.all_gather(jnp.concatenate([levels[0], levels[1], new_keyval], 0), 'm...]
    all_to_all x1, waiting for transfers between devices: 92.6 us -> 16.6 us  [body(): lax.all_to_all(outgoing, 'req', split_axis=0, concat_axis=0, tiled=True)]
    dot_general x9 -> x1, matrix products: 58.6 us -> 0.77 us  [body(): jnp.einsum('rln,lnsc->rlsc', picker, shared_rows, preferred_element_type=...]
    reduce_scatter x1 -> x0, waiting for transfers between devices: 36.6 us -> none  [body(): lax.psum_scatter(lax.dot_general(hidden, down_full, (((1,), (1,)), ((), (...]
    reduce_sum x2 -> x0, other arithmetic: 14.4 us -> none  [attend(): return (top, jnp.sum(weights, axis=-1), mixed)]
    dynamic_update_slice x0 -> x4, local copies, waits for them, and re-layouts: none -> 7.74 us  [the longest x1 3.03 us: body(): lax.dynamic_update_slice(laid, gathered[:, 2 * share:].reshape(groups * t...]
    all_gather x1 -> x0, blocking collectives: 7.17 us -> none  [body(): piece = lax.all_gather(new_keyval, 'mlp', axis=0, tiled=True)]
  transfers between devices with their start and end apart: 6 -> 2, of which waited for: 5 -> 2; matrix products, arithmetic and copies ran while one was open for 20% -> 5% of each run, Pallas kernels for 0% -> 0%
where the time goes in v1:
time: 233 us; the launch traced here: 232 us
  Pallas kernels  149 us (64%)
  waiting for transfers between devices  23.2 us (10%)
  between operations  21.3 us (9%)
  local copies, waits for them, and re-layouts  20 us (9%)
  starting transfers between devices  7.47 us (3%)
  matrix products  5.69 us (2%)
  other arithmetic  5.18 us (2%)
    pallas_call x1, Pallas kernels, fused_layer(): pl.pallas_call(functools.partial(layer_kernel, (n_req, n_mlp)), out_shape...  149 us
    all_to_all x1, waiting for transfers between devices, body(): lax.all_to_all(outgoing, 'req', split_axis=0, concat_axis=0, tiled=True)  16.6 us
    all_to_all x1, starting transfers between devices, body(): lax.all_to_all(outgoing, 'req', split_axis=0, concat_axis=0, tiled=True)  7.43 us
    all_gather x1, waiting for transfers between devices, body(): lax.all_gather(jnp.concatenate([levels[0], levels[1], new_keyval], 0), 'm...  6.54 us
  transfers between devices with their start and end apart: 2, of which 2 were waited for; matrix products, arithmetic and copies ran while one was open for 5% of the time, Pallas kernels for 0%

profile of v1, /device:TPU:0, one launch (start us, length us, event | category | flops | bytes accessed | tf_op | source)
XLA Modules:
  0.0 231.8 jit_solution(9141151582934912173)
XLA Ops:
  6.5 0.7 compare_select_fusion
  7.3 1.3 gather_fusion
  8.6 0.7 and_select_fusion.1
  9.3 0.7 fusion.26
  9.9 1.3 constant_dynamic-slice_fusion.1
  11.3 0.8 fusion.4
  12.0 1.2 copy.26
  13.2 7.4 %all-to-all-start = ((bf16[8,2,128,256]{3,2,1,0:T(8,128)(2,1)}), bf16[8,2,128,256]{3,2,1,0:T(8,128)(2,1)S(1)}, u32[]{:S(2)}, u32[]{:S(2)}) async-start(bf16[8,2,128,256]{3,2,1,0:T(8,128)(2,1)} %copy.26), calls=%async_computation | async-start | bytes 2097152 | tf_op jit(solution)/shard_map/all_to_all | solution.py:349
  20.7 0.6 dynamic_slice.24
  23.3 0.6 dynamic_slice.25
  25.2 0.2 fusion
  25.4 0.6 fusion.6
  26.7 0.7 constant_dynamic-slice_fusion.3
  29.3 0.2 fusion.25
  29.5 0.3 fusion.15
  29.8 16.6 %all-to-all-done = bf16[8,2,128,256]{3,2,1,0:T(8,128)(2,1)S(1)} async-done(((bf16[8,2,128,256]{3,2,1,0:T(8,128)(2,1)}), bf16[8,2,128,256]{3,2,1,0:T(8,128)(2,1)S(1)}, u32[]{:S(2)}, u32[]{:S(2)}) %all-to-all-start) | async-done | bytes 1048608 | tf_op jit(solution)/shard_map/all_to_all | solution.py:349
  46.4 0.3 multiply_reduce_fusion
  46.8 0.7 maximum_maximum_fusion
  49.5 0.3 multiply_cosine_fusion.1
  49.8 4.4 %fusion.8 = f32[256,1536]{0,1:T(8,128)S(1)} fusion(bf16[1536,1536]{1,0:T(8,128)(2,1)} %param.16, bf16[256,1536]{1,0:T(8,128)(2,1)S(1)} %copy-done.2, f32[1536]{0:T(1024)S(1)} %copy-done.6, f32[256]{0:T(256)S(1)} %add_rsqrt_fusion), kind=kOutput, calls=%fused_computation.16 | convolution fusion | flops 1209532416 | bytes 7085056 | tf_op jit(solution)/shard_map/dot_general | solution.py:357
  54.2 0.2 multiply_subtract_fusion
  54.6 1.2 copy.29.q_ref
  55.7 0.6 broadcast_in_dim.8.gain_ref
  56.3 0.6 compare_convert_fusion.ok_ref
  56.9 6.5 %all-gather.3.cloned.1.call-done = bf16[2048,256]{0,1:T(8,128)(2,1)} async-done(((bf16[512,256]{0,1:T(8,128)(2,1)}), bf16[2048,256]{0,1:T(8,128)(2,1)}) %all-gather.3.cloned.1.call-update) | async-done | bytes 1048592 | tf_op jit(solution)/shard_map/all_gather | solution.py:365
  63.5 1.5 copy.39
  65.2 1.9 dynamic_update_slice.13
  67.1 2.7 %dynamic_update_slice.14 = bf16[3584,256]{1,0:T(8,128)(2,1)S(1)} dynamic-update-slice(bf16[3584,256]{1,0:T(8,128)(2,1)S(1)} %dynamic_update_slice.13, bf16[512,256]{1,0:T(8,128)(2,1)} %bitcast.45, s32[]{:T(128)S(6)} %select_n.68, s32[]{:T(128)} %constant.64.clone.1) | dynamic-update-slice | bytes 524292 | tf_op jit(solution)/shard_map/dynamic_update_slice | solution.py:374
  69.8 3.0 %dynamic_update_slice.15 = bf16[3584,256]{1,0:T(8,128)(2,1)S(1)} dynamic-update-slice(bf16[3584,256]{1,0:T(8,128)(2,1)S(1)} %dynamic_update_slice.14, bf16[1024,256]{1,0:T(8,128)(2,1)S(1)} %bitcast.40, s32[]{:T(128)S(6)} %select_n.69, s32[]{:T(128)} %constant.64.clone.1) | dynamic-update-slice | bytes 1048580 | tf_op jit(solution)/shard_map/dynamic_update_slice | solution.py:375
  72.9 1.0 constant_dynamic-slice_fusion.kv_ref
  73.9 149.0 %shard_map.136 = bf16[256,1536]{1,0:T(8,128)(2,1)} custom-call(bf16[256,1536]{1,0:T(8,128)(2,1)} %copy.29.q_ref, bf16[1280,256]{1,0:T(8,128)(2,1)} %constant_dynamic-slice_fusion.kv_ref, s32[1,1280]{1,0:T(1,128)} %compare_convert_fusion.ok_ref, bf16[256,1536]{1,0:T(8,128)(2,1)} %tok_ref.1, f32[1,1536]{1,0:T(1,128)} %broadcast_in_dim.8.gain_ref, ...), custom_call_target="tpu_custom_call" | custom-call | tf_op jit(solution)/shard_map/pallas_call | solution.py:284
  222.9 2.1 copy.48
  (30 shorter events, 0.7 us)
Async XLA Ops:
  6.5 18.9 %copy-start = (bf16[1536,256]{1,0:T(8,128)(2,1)S(1)}, bf16[1536,256]{1,0:T(8,128)(2,1)}, u32[]{:S(2)}) copy-start(bf16[1536,256]{1,0:T(8,128)(2,1)} %param.17) | copy-start | bytes 2359300
  13.2 7.5 %copy-start.4 = (s32[8]{0:T(128)S(1)}, s32[8]{0:T(128)}, u32[]{:S(2)}) copy-start(s32[8]{0:T(128)} %param.25) | copy-start | bytes 100
  13.2 10.0 %copy-start.1 = (s32[64]{0:T(128)S(1)}, s32[64]{0:T(128)}, u32[]{:S(2)}) copy-start(s32[64]{0:T(128)} %param.26) | copy-start | bytes 772
  13.2 11.9 %copy-start.2 = (bf16[256,1536]{1,0:T(8,128)(2,1)S(1)}, bf16[256,1536]{1,0:T(8,128)(2,1)}, u32[]{:S(2)}) copy-start(bf16[256,1536]{1,0:T(8,128)(2,1)} %tok_ref.1) | copy-start | bytes 2359300
  13.2 12.2 %copy-start.6 = (f32[1536]{0:T(1024)S(1)}, f32[1536]{0:T(1024)}, u32[]{:S(2)}) copy-start(f32[1536]{0:T(1024)} %param.15) | copy-start | bytes 18436
  13.2 33.2 %all-to-all-start = ((bf16[8,2,128,256]{3,2,1,0:T(8,128)(2,1)}), bf16[8,2,128,256]{3,2,1,0:T(8,128)(2,1)S(1)}, u32[]{:S(2)}, u32[]{:S(2)}) async-start(bf16[8,2,128,256]{3,2,1,0:T(8,128)(2,1)} %copy.26), calls=%async_computation | async-start | bytes 2097152 | tf_op jit(solution)/shard_map/all_to_all | solution.py:349
  20.7 6.0 %copy-start.5 = (s32[3,64]{1,0:T(4,128)S(1)}, s32[3,64]{1,0:T(4,128)}, u32[]{:S(2)}) copy-start(s32[3,64]{1,0:T(4,128)} %param.27) | copy-start | bytes 2308
  20.7 42.8 %all-gather.3.cloned.1.call-start = ((), (), s32[]{:S(2)}) async-start(), calls=%async_computation.1 | async-start | bytes 1310720 | tf_op jit(solution)/shard_map/all_gather | solution.py:365
  54.4 1.4 copy-start.3
Sparse Core Ops, SparseCore 0:
  47.7 15.7 all-gather.2

commit v2 on v1

--- a/solution.py
+++ b/solution.py
@@ -33,12 +33,23 @@
 
 LINE = 4
 MASKED = -1e30
+N_EARLY = 10
 
 
 def layer_kernel(
-    dims, q_ref, kv_ref, ok_ref, tok_ref, gain_ref, wout_hbm, wg_hbm, wu_hbm, wd_hbm, out_ref,
-    w_all, w_out, bias, ctx, rows_all, hidden, part, landed,
-    load_sem, zs, zr, ys, yr, ts, tr, ps, pr,
+    dims, q_ref, kv_ref, ok_ref, tok_ref, gain_ref, wout_hbm, wg_hbm, wu_hbm, wd_hbm, *rest
+):
+    early, rest = rest[:N_EARLY * dims[2]], rest[N_EARLY * dims[2]:]
+    layer_steps(
+        dims[:2], early, q_ref, kv_ref, ok_ref, tok_ref, gain_ref, wout_hbm, wg_hbm, wu_hbm,
+        wd_hbm, *rest
+    )
+
+
+def layer_steps(
+    dims, early, q_ref, kv_ref, ok_ref, tok_ref, gain_ref, wout_hbm, wg_hbm, wu_hbm, wd_hbm,
+    out_ref, w_all, w_out, bias, ctx, rows_all, hidden, part, landed,
+    load_sem, zs, zr, ys, yr, ts, tf, tr, ps, pr,
 ):
     n_req, n_mlp = dims
     cross = n_req // LINE
@@ -58,6 +69,23 @@
     for load in loads:
         load.start()
 
+    ready = []
+    for i, src in enumerate(early):
+        kind = EARLY_BLOCKS[i]
+        for j in range(src.shape[0]):
+            a, b = za + kind[1], (1 - yb if kind[2] else yb)
+            place = jnp.clip(a, 0, LINE - 1) * cross + b
+            copy = pltpu.make_async_copy(
+                src.at[j],
+                w_all.at[kind[0] + j, pl.ds(pl.multiple_of(place * depth, 16), depth)],
+                load_sem.at[4 + 2 * i + j],
+            )
+            ready.append(((a >= 0) & (a < LINE), copy))
+    for there, copy in ready:
+        @pl.when(there)
+        def _():
+            copy.start()
+
     barrier = pltpu.get_barrier_semaphore()
     for k in range(1, LINE):
         pl.semaphore_signal(barrier, inc=1, device_id={"req": ((za + k) % LINE) * cross + yb})
@@ -108,12 +136,17 @@
 
             @pl.when((origin >= 0) & (origin < LINE))
             def _():
-                if not finish:
+                if not (finish or (early and (dist == 1 or (w == 0 and dist == 2)))):
                     z_copy(w, origin, za, 0).wait_recv()
                 z_send(w, origin, (-side,), finish)
                 y_send(w, origin, yb, (-1, 1), finish)
 
     def y_wait(w, a):
+        if early:
+            @pl.when(jnp.abs(a - za) > (1 if w == 0 else 0))
+            def _():
+                y_copy(w, a, 1 - yb, yb, 0).wait_recv()
+            return
         for dist in range(1, cross):
             for side in (-1, 1):
                 origin = yb + side * dist
@@ -125,8 +158,16 @@
 
     for load in loads[:3]:
         load.wait()
-    own(0)
-    own(1)
+    for there, copy in ready:
+        @pl.when(there)
+        def _():
+            copy.wait()
+    if early:
+        relay(1, 1)
+        relay(0, 2)
+    else:
+        own(0)
+        own(1)
 
     query_row = lax.broadcasted_iota(jnp.int32, (tok, keys), 0)
     slot = lax.broadcasted_iota(jnp.int32, (tok, keys), 1)
@@ -150,12 +191,19 @@
 
     third = HEADS // 3
     heads(0, third)
-    relay(0, 1)
+    if early:
+        relay(2, 1)
+    else:
+        relay(0, 1)
+        relay(1, 1)
     heads(third, third)
-    relay(1, 1)
-    own(2)
+    if early:
+        relay(1, 2)
+    else:
+        own(2)
+        relay(0, 2)
     heads(2 * third, HEADS - 2 * third)
-    relay(0, 2)
+    relay(0, 3) if early else relay(1, 2)
     loads[3].wait()
 
     @pl.loop(0, LINE)
@@ -168,20 +216,29 @@
 
     rows_all[mine] = rms_scale(out_ref[...], gain_ref[...]).astype(jnp.bfloat16)
 
-    def t_copy(owner, toward):
+    def t_copy(owner, toward, sem):
         return pltpu.make_async_remote_copy(
             src_ref=rows_all.at[owner], dst_ref=rows_all.at[owner],
-            send_sem=ts.at[toward], recv_sem=tr.at[owner], device_id={"mlp": toward},
+            send_sem=sem, recv_sem=tr.at[owner], device_id={"mlp": toward},
         )
 
     others = [(mine + k) % n_mlp for k in range(1, n_mlp)]
-    for toward in others:
-        t_copy(mine, toward).start()
-    relay(1, 2)
-    relay(2, 1)
-    relay(0, 3)
-    relay(1, 3)
-    relay(2, 2)
+    core = mine % 2
+    sibling = mine + 1 - 2 * core
+    alike = [(mine + 2 * k) % n_mlp for k in range(1, n_mlp // 2)]
+    for toward in alike + [sibling]:
+        t_copy(mine, toward, ts.at[toward]).start()
+    if early:
+        relay(2, 2)
+        relay(1, 3)
+    else:
+        relay(2, 1)
+        relay(0, 3)
+        relay(1, 3)
+        relay(2, 2)
+    for owner in alike:
+        t_copy(owner, mine, ts.at[0]).wait_recv()
+        t_copy(owner, sibling, tf.at[owner]).start()
     for w in range(2):
         for a in range(LINE):
             y_wait(w, a)
@@ -196,17 +253,16 @@
             upward = jnp.dot(rows_all[g], w_all[1, :, cols], preferred_element_type=jnp.float32)
             hidden[g, :, cols] = (jax.nn.gelu(gate, approximate=True) * upward).astype(jnp.bfloat16)
 
-    @pl.loop(0, n_mlp)
+    gate_up(mine)
+    for g in alike:
+        gate_up(g)
+    relay(2, 3)
+
+    @pl.loop(0, n_mlp // 2)
     def _(k):
-        g = (mine + k) % n_mlp
-
-        @pl.when(k > 0)
-        def _():
-            t_copy(g, mine).wait_recv()
-
+        g = (sibling + 2 * k) % n_mlp
+        t_copy(g, mine, ts.at[0]).wait_recv()
         gate_up(g)
-
-    relay(2, 3)
 
     def p_copy(g, src, c):
         return pltpu.make_async_remote_copy(
@@ -247,32 +303,62 @@
             total = total + landed[g, a].astype(jnp.float32)
         out_ref[:, cols] = (out_ref[:, cols].astype(jnp.float32) + total).astype(jnp.bfloat16)
 
-    for toward in others:
-        t_copy(mine, toward).wait_send()
+    for toward in alike + [sibling]:
+        t_copy(mine, toward, ts.at[toward]).wait_send()
+    for owner in alike:
+        t_copy(owner, sibling, tf.at[owner]).wait_send()
 
     @pl.loop(0, LINE)
     def _(a):
         for g in others:
             p_copy(g, mine, a).wait_send()
 
-    @pl.loop(0, 3)
-    def _(w):
-        own(w, True)
-        for dist in range(1, LINE):
+    for w in range(3):
+        if not early:
+            own(w, True)
+        for dist in range(2 if early and w == 0 else 1, LINE):
             relay(w, dist, True)
-
-        @pl.loop(0, LINE)
-        def _(a):
-            for dist in range(1, cross):
-                for side in (-1, 1):
-                    origin = yb + side * dist
-
-                    @pl.when((origin >= 0) & (origin < cross))
-                    def _():
-                        y_send(w, a, origin, (-side,), True)
-
-
-def fused_layer(n_req, n_mlp, q, kv, ok, tokens, gain, w_out, w_gate, w_up, w_down):
+    if not early:
+        @pl.loop(0, 3)
+        def _(w):
+            @pl.loop(0, LINE)
+            def _(a):
+                for dist in range(1, cross):
+                    for side in (-1, 1):
+                        origin = yb + side * dist
+
+                        @pl.when((origin >= 0) & (origin < cross))
+                        def _():
+                            y_send(w, a, origin, (-side,), True)
+
+
+EARLY_BLOCKS = [
+    (0, 0, 1), (0, -1, 0), (0, 1, 0), (1, 0, 1), (1, -1, 0), (1, 1, 0),
+    (0, -1, 1), (0, 1, 1), (0, -2, 0), (0, 2, 0),
+]
+
+
+def early_blocks(w_gate, w_up, w_down):
+    requests = lax.axis_size("req")
+    cross = requests // LINE
+    if cross != 2:
+        return []
+    swap = [(r, r ^ 1) for r in range(requests)]
+    ahead = [(r, r + cross) for r in range(requests - cross)]
+    back = [(r + cross, r) for r in range(requests - cross)]
+    send = functools.partial(lax.ppermute, axis_name="req")
+    gate = w_gate[None]
+    pair = jnp.stack([w_up, w_down])
+    gate_low, gate_high = send(gate, perm=ahead), send(gate, perm=back)
+    return [
+        send(gate, perm=swap), gate_low, gate_high,
+        send(pair, perm=swap), send(pair, perm=ahead), send(pair, perm=back),
+        send(gate_low, perm=swap), send(gate_high, perm=swap),
+        send(gate_low, perm=ahead), send(gate_high, perm=back),
+    ]
+
+
+def fused_layer(n_req, n_mlp, q, kv, ok, tokens, gain, w_out, w_gate, w_up, w_down, early):
     tok, model = tokens.shape
     depth, width = w_gate.shape
     chunk = model // LINE
@@ -282,9 +368,9 @@
     dma = pltpu.SemaphoreType.DMA
     half = jnp.bfloat16
     return pl.pallas_call(
-        functools.partial(layer_kernel, (n_req, n_mlp)),
+        functools.partial(layer_kernel, (n_req, n_mlp, int(len(early) > 0))),
         out_shape=jax.ShapeDtypeStruct((tok, model), half),
-        in_specs=[whole] * 5 + [far] * 4,
+        in_specs=[whole] * 5 + [far] * (4 + len(early)),
         out_specs=whole,
         scratch_shapes=[
             pltpu.VMEM((3, model, width), half),
@@ -295,11 +381,12 @@
             pltpu.VMEM((n_mlp, tok, width), half),
             pltpu.VMEM((n_mlp, LINE, tok, chunk), half),
             pltpu.VMEM((n_mlp, LINE, tok, chunk), half),
-            dma((4,)),
+            dma((4 + 2 * N_EARLY,)),
             dma((3, LINE, 2)),
             dma((3, LINE)),
             dma((3, LINE, cross, 2)),
             dma((3, LINE, cross)),
+            dma((n_mlp,)),
             dma((n_mlp,)),
             dma((n_mlp,)),
             dma((n_mlp, LINE)),
@@ -308,7 +395,7 @@
         compiler_params=pltpu.CompilerParams(
             collective_id=0, has_side_effects=True, vmem_limit_bytes=58 * 1024 * 1024
         ),
-    )(q, kv, ok, tokens, gain, w_out, w_gate, w_up, w_down)
+    )(q, kv, ok, tokens, gain, w_out, w_gate, w_up, w_down, *early)
 
 
 def body(
@@ -329,6 +416,8 @@
     len_two = seg_lengths[2, mine]
     total = len_zero + len_one + len_two
 
+    early = early_blocks(w_gate, w_up, w_down)
+
     share = seg_slot // groups
     level_zero = node_parent[leaf_parent]
     wanted = jnp.stack([level_zero, leaf_parent], 1)
@@ -381,7 +470,7 @@
     used = (first - WINDOW + jnp.arange(keys, dtype=jnp.int32) >= 0).astype(jnp.int32)[None, :]
     return fused_layer(
         requests, groups, queries.reshape(tok_rows, HEADS * HD), window, used, tokens,
-        ffn_gain[None, :], w_out, w_gate, w_up, w_down,
+        ffn_gain[None, :], w_out, w_gate, w_up, w_down, early,
     )
 
 

time: 233 us -> 240 us (1.030)
  Pallas kernels: 149 us -> 118 us
  starting transfers between devices: 7.47 us -> 24.6 us
  waiting for transfers between devices: 23.2 us -> 36.9 us
  local copies, waits for them, and re-layouts: 20 us -> 23.3 us
  other arithmetic: 5.18 us -> 8.34 us
    pallas_call x1, Pallas kernels: 149 us -> 118 us  [fused_layer(): pl.pallas_call(functools.partial(layer_kernel, (n_req, n_mlp, int(len(ear...]
    ppermute x0 -> x10, waiting for transfers between devices: none -> 27.3 us  [the longest x1 17 us: early_blocks(): send(gate, perm=swap)]
    ppermute x0 -> x10, starting transfers between devices: none -> 17.2 us  [the longest x2 6.06 us: early_blocks(): gate_low, gate_high = (send(gate, perm=ahead), send(gate, perm=back))]
    all_to_all x1, waiting for transfers between devices: 16.6 us -> 9.61 us  [body(): lax.all_to_all(outgoing, 'req', split_axis=0, concat_axis=0, tiled=True)]
    all_gather x1, waiting for transfers between devices: 6.54 us -> 0.01 us  [body(): lax.all_gather(jnp.concatenate([levels[0], levels[1], new_keyval], 0), 'm...]
  transfers between devices with their start and end apart: 2 -> 12, of which waited for: 2 -> 5; matrix products, arithmetic and copies ran while one was open for 5% -> 12% of each run, Pallas kernels for 0% -> 0%
where the time goes in v2:
time: 240 us; the launch traced here: 238 us
  Pallas kernels  118 us (49%)
  waiting for transfers between devices  36.9 us (15%)
  starting transfers between devices  24.6 us (10%)
  local copies, waits for them, and re-layouts  23.3 us (10%)
  between operations  20.9 us (9%)
  other arithmetic  8.34 us (3%)
  matrix products  5.68 us (2%)
    pallas_call x1, Pallas kernels, fused_layer(): pl.pallas_call(functools.partial(layer_kernel, (n_req, n_mlp, int(len(ear...  118 us
    ppermute x1, waiting for transfers between devices, early_blocks(): send(gate, perm=swap)  17 us
    all_to_all x1, waiting for transfers between devices, body(): lax.all_to_all(outgoing, 'req', split_axis=0, concat_axis=0, tiled=True)  9.61 us
    all_to_all x1, starting transfers between devices, body(): lax.all_to_all(outgoing, 'req', split_axis=0, concat_axis=0, tiled=True)  7.43 us
    ppermute x1, waiting for transfers between devices, early_blocks(): send(gate_low, perm=swap)  6.21 us
    ppermute x2, starting transfers between devices, early_blocks(): gate_low, gate_high = (send(gate, perm=ahead), send(gate, perm=back))  6.06 us
  transfers between devices with their start and end apart: 12, of which 5 were waited for; matrix products, arithmetic and copies ran while one was open for 12% of the time, Pallas kernels for 0%

profile of v2, /device:TPU:0, one launch (start us, length us, event | category | flops | bytes accessed | tf_op | source)
XLA Modules:
  0.0 237.6 jit_solution(2723546483918483559)
XLA Ops:
  7.3 1.3 gather_fusion
  9.9 1.3 constant_dynamic-slice_fusion.1
  12.0 1.2 copy.26
  13.3 7.4 %all-to-all-start = ((bf16[8,2,128,256]{3,2,1,0:T(8,128)(2,1)}), bf16[8,2,128,256]{3,2,1,0:T(8,128)(2,1)S(1)}, u32[]{:S(2)}, u32[]{:S(2)}) async-start(bf16[8,2,128,256]{3,2,1,0:T(8,128)(2,1)} %copy.26), calls=%async_computation | async-start | bytes 2097152 | tf_op jit(solution)/shard_map/all_to_all | solution.py:438
  20.7 4.8 %collective-permute-start.1 = (bf16[1,192,1152]{2,1,0:T(8,128)(2,1)}, bf16[1,192,1152]{2,1,0:T(8,128)(2,1)}, u32[]{:S(2)}, u32[]{:S(2)}) collective-permute-start(bf16[1,192,1152]{2,1,0:T(8,128)(2,1)} %bitcast.23), channel_id=1, source_target_pairs={{0,8},{4,12},{8,16},{12,20},{16,24},{20,28},{1,9},{5,13},{9,17},{1... | collective-permute-start | bytes 1327112 | tf_op jit(solution)/shard_map/ppermute | solution.py:352
  25.5 1.3 collective-permute-start.2
  36.4 0.9 slice_bitcast_fusion
  38.3 9.6 %all-to-all-done = bf16[8,2,128,256]{3,2,1,0:T(8,128)(2,1)S(1)} async-done(((bf16[8,2,128,256]{3,2,1,0:T(8,128)(2,1)}), bf16[8,2,128,256]{3,2,1,0:T(8,128)(2,1)S(1)}, u32[]{:S(2)}, u32[]{:S(2)}) %all-to-all-start) | async-done | bytes 1048608 | tf_op jit(solution)/shard_map/all_to_all | solution.py:438
  47.9 0.9 multiply_reduce_fusion
  48.8 1.0 copy.38
  49.9 1.6 maximum_maximum_fusion
  51.5 1.0 pad_maximum_fusion
  52.5 1.0 collective-permute-start.3
  53.5 2.2 collective-permute-start.4
  55.8 1.0 collective-permute-start
  56.8 4.3 %fusion.8 = f32[256,1536]{0,1:T(8,128)S(1)} fusion(bf16[1536,1536]{1,0:T(8,128)(2,1)} %param.16, bf16[256,1536]{1,0:T(8,128)(2,1)S(1)} %copy-done.2, f32[1536]{0:T(1024)S(1)} %copy-done.11, f32[256]{0:T(256)S(1)} %add_rsqrt_fusion), kind=kOutput, calls=%fused_computation.17 | convolution fusion | flops 1209532416 | bytes 7085056 | tf_op jit(solution)/shard_map/dot_general | solution.py:446
  63.6 1.2 copy.29.q_ref
  65.4 1.3 collective-permute-start.5
  66.7 1.2 collective-permute-start.6
  67.9 17.0 %collective-permute-done.rest_0_ = bf16[1,192,1152]{2,1,0:T(8,128)(2,1)} collective-permute-done((bf16[1,192,1152]{2,1,0:T(8,128)(2,1)}, bf16[1,192,1152]{2,1,0:T(8,128)(2,1)}, u32[]{:S(2)}, u32[]{:S(2)}) %collective-permute-start) | collective-permute-done | bytes 442400 | tf_op jit(solution)/shard_map/ppermute | solution.py:354
  84.9 1.0 collective-permute-start.7
  86.5 1.5 copy.39
  88.1 6.2 %collective-permute-done.6.rest_6_ = bf16[1,192,1152]{2,1,0:T(8,128)(2,1)S(1)} collective-permute-done((bf16[1,192,1152]{2,1,0:T(8,128)(2,1)}, bf16[1,192,1152]{2,1,0:T(8,128)(2,1)S(1)}, u32[]{:S(2)}, u32[]{:S(2)}) %collective-permute-start.6) | collective-permute-done | bytes 442400 | tf_op jit(solution)/shard_map/ppermute | solution.py:356
  94.3 2.1 collective-permute-start.8
  96.4 3.6 %collective-permute-done.7.rest_7_ = bf16[1,192,1152]{2,1,0:T(8,128)(2,1)S(1)} collective-permute-done((bf16[1,192,1152]{2,1,0:T(8,128)(2,1)}, bf16[1,192,1152]{2,1,0:T(8,128)(2,1)S(1)}, u32[]{:S(2)}, u32[]{:S(2)}) %collective-permute-start.7) | collective-permute-done | bytes 442400 | tf_op jit(solution)/shard_map/ppermute | solution.py:356
  100.0 1.3 collective-permute-start.9
  101.5 2.1 dynamic_update_slice.13
  103.6 2.7 %dynamic_update_slice.14 = bf16[3584,256]{1,0:T(8,128)(2,1)S(1)} dynamic-update-slice(bf16[3584,256]{1,0:T(8,128)(2,1)S(1)} %dynamic_update_slice.13, bf16[512,256]{1,0:T(8,128)(2,1)} %bitcast.50, s32[]{:T(128)S(6)} %select_n.68, s32[]{:T(128)} %constant.64.clone.1) | dynamic-update-slice | bytes 524292 | tf_op jit(solution)/shard_map/dynamic_update_slice | solution.py:463
  106.3 3.0 %dynamic_update_slice.15 = bf16[3584,256]{1,0:T(8,128)(2,1)S(1)} dynamic-update-slice(bf16[3584,256]{1,0:T(8,128)(2,1)S(1)} %dynamic_update_slice.14, bf16[1024,256]{1,0:T(8,128)(2,1)S(1)} %bitcast.43, s32[]{:T(128)S(6)} %select_n.69, s32[]{:T(128)} %constant.64.clone.1) | dynamic-update-slice | bytes 1048580 | tf_op jit(solution)/shard_map/dynamic_update_slice | solution.py:464
  109.3 1.0 constant_dynamic-slice_fusion.kv_ref
  110.7 117.9 %shard_map.136 = bf16[256,1536]{1,0:T(8,128)(2,1)} custom-call(bf16[256,1536]{1,0:T(8,128)(2,1)} %copy.29.q_ref, bf16[1280,256]{1,0:T(8,128)(2,1)} %constant_dynamic-slice_fusion.kv_ref, s32[1,1280]{1,0:T(1,128)} %compare_convert_fusion.ok_ref, bf16[256,1536]{1,0:T(8,128)(2,1)} %tok_ref.1, f32[1,1536]{1,0:T(1,128)} %broadcast_in_dim.10.gain_ref, ...), custom_call_target="tpu_custom_call" | custom-call | tf_op jit(solution)/shard_map/pallas_call | solution.py:370
  228.7 2.1 copy.48
  (61 shorter events, 10.5 us)
Async XLA Ops:
  6.5 24.8 %copy-start = (bf16[1536,256]{1,0:T(8,128)(2,1)S(1)}, bf16[1536,256]{1,0:T(8,128)(2,1)}, u32[]{:S(2)}) copy-start(bf16[1536,256]{1,0:T(8,128)(2,1)} %param.17) | copy-start | bytes 2359300
  13.2 13.6 %copy-start.9 = (s32[8]{0:T(128)S(1)}, s32[8]{0:T(128)}, u32[]{:S(2)}) copy-start(s32[8]{0:T(128)} %param.25) | copy-start | bytes 100
  13.3 16.1 %copy-start.1 = (s32[64]{0:T(128)S(1)}, s32[64]{0:T(128)}, u32[]{:S(2)}) copy-start(s32[64]{0:T(128)} %param.26) | copy-start | bytes 772
  13.3 17.8 %copy-start.2 = (bf16[256,1536]{1,0:T(8,128)(2,1)S(1)}, bf16[256,1536]{1,0:T(8,128)(2,1)}, u32[]{:S(2)}) copy-start(bf16[256,1536]{1,0:T(8,128)(2,1)} %tok_ref.1) | copy-start | bytes 2359300
  13.3 18.1 %copy-start.11 = (f32[1536]{0:T(1024)S(1)}, f32[1536]{0:T(1024)}, u32[]{:S(2)}) copy-start(f32[1536]{0:T(1024)} %param.15) | copy-start | bytes 18436
  13.3 34.7 %all-to-all-start = ((bf16[8,2,128,256]{3,2,1,0:T(8,128)(2,1)}), bf16[8,2,128,256]{3,2,1,0:T(8,128)(2,1)S(1)}, u32[]{:S(2)}, u32[]{:S(2)}) async-start(bf16[8,2,128,256]{3,2,1,0:T(8,128)(2,1)} %copy.26), calls=%async_computation | async-start | bytes 2097152 | tf_op jit(solution)/shard_map/all_to_all | solution.py:438
  20.7 13.2 %copy-start.10 = (s32[3,64]{1,0:T(4,128)S(1)}, s32[3,64]{1,0:T(4,128)}, u32[]{:S(2)}) copy-start(s32[3,64]{1,0:T(4,128)} %param.27) | copy-start | bytes 2308
  20.7 65.8 %all-gather.3.cloned.1.call-start = ((), (), s32[]{:S(2)}) async-start(), calls=%async_computation.1 | async-start | bytes 1310720 | tf_op jit(solution)/shard_map/all_gather | solution.py:454
  20.7 44.6 %collective-permute-start.1 = (bf16[1,192,1152]{2,1,0:T(8,128)(2,1)}, bf16[1,192,1152]{2,1,0:T(8,128)(2,1)}, u32[]{:S(2)}, u32[]{:S(2)}) collective-permute-start(bf16[1,192,1152]{2,1,0:T(8,128)(2,1)} %bitcast.23), channel_id=1, source_target_pairs={{0,8},{4,12},{8,16},{12,20},{16,24},{20,28},{1,9},{5,13},{9,17},{1... | collective-permute-start | bytes 1327112 | tf_op jit(solution)/shard_map/ppermute | solution.py:352
  25.5 41.1 %collective-permute-start.2 = (bf16[1,192,1152]{2,1,0:T(8,128)(2,1)}, bf16[1,192,1152]{2,1,0:T(8,128)(2,1)}, u32[]{:S(2)}, u32[]{:S(2)}) collective-permute-start(bf16[1,192,1152]{2,1,0:T(8,128)(2,1)} %bitcast.23), channel_id=1, source_target_pairs={{8,0},{12,4},{16,8},{20,12},{24,16},{28,20},{9,1},{13,5},{17,9},{2... | collective-permute-start | bytes 1327112 | tf_op jit(solution)/shard_map/ppermute | solution.py:352
  31.9 0.7 copy-start.7
  33.3 18.3 %copy-start.3 = (bf16[192,1152]{1,0:T(8,128)(2,1)S(1)}, bf16[192,1152]{1,0:T(8,128)(2,1)}, u32[]{:S(2)}) copy-start(bf16[192,1152]{1,0:T(8,128)(2,1)} %wu_hbm.1) | copy-start | bytes 1327108
  33.3 18.3 %copy-start.4 = (bf16[192,1152]{1,0:T(8,128)(2,1)S(1)}, bf16[192,1152]{1,0:T(8,128)(2,1)}, u32[]{:S(2)}) copy-start(bf16[192,1152]{1,0:T(8,128)(2,1)} %wd_hbm.1) | copy-start | bytes 1327108
  52.5 58.2 %collective-permute-start.3 = (bf16[2,192,1152]{2,1,0:T(8,128)(2,1)}, bf16[2,192,1152]{2,1,0:T(8,128)(2,1)}, u32[]{:S(2)}, u32[]{:S(2)}) collective-permute-start(bf16[2,192,1152]{2,1,0:T(8,128)(2,1)} %pad_maximum_fusion), channel_id=1, source_target_pairs={{0,4},{4,0},{8,12},{12,8},{16,20},{20,16},{24,28},{28,24},{1,5},{5... | collective-permute-start | bytes 2654216 | tf_op jit(solution)/shard_map/ppermute | solution.py:355
  53.5 57.2 %collective-permute-start.4 = (bf16[2,192,1152]{2,1,0:T(8,128)(2,1)}, bf16[2,192,1152]{2,1,0:T(8,128)(2,1)}, u32[]{:S(2)}, u32[]{:S(2)}) collective-permute-start(bf16[2,192,1152]{2,1,0:T(8,128)(2,1)} %pad_maximum_fusion), channel_id=1, source_target_pairs={{0,8},{4,12},{8,16},{12,20},{16,24},{20,28},{1,9},{5,13},{9,17},{1... | collective-permute-start | bytes 2654216 | tf_op jit(solution)/shard_map/ppermute | solution.py:355
  55.8 29.2 %collective-permute-start = (bf16[1,192,1152]{2,1,0:T(8,128)(2,1)}, bf16[1,192,1152]{2,1,0:T(8,128)(2,1)}, u32[]{:S(2)}, u32[]{:S(2)}) collective-permute-start(bf16[1,192,1152]{2,1,0:T(8,128)(2,1)} %bitcast.23), channel_id=1, source_target_pairs={{0,4},{4,0},{8,12},{12,8},{16,20},{20,16},{24,28},{28,24},{1,5},{5... | collective-permute-start | bytes 1327112 | tf_op jit(solution)/shard_map/ppermute | solution.py:354
  63.4 1.4 copy-start.8
  65.4 45.4 %collective-permute-start.5 = (bf16[2,192,1152]{2,1,0:T(8,128)(2,1)}, bf16[2,192,1152]{2,1,0:T(8,128)(2,1)}, u32[]{:S(2)}, u32[]{:S(2)}) collective-permute-start(bf16[2,192,1152]{2,1,0:T(8,128)(2,1)} %pad_maximum_fusion), channel_id=1, source_target_pairs={{8,0},{12,4},{16,8},{20,12},{24,16},{28,20},{9,1},{13,5},{17,9},{2... | collective-permute-start | bytes 2654216 | tf_op jit(solution)/shard_map/ppermute | solution.py:355
  66.7 27.6 %collective-permute-start.6 = (bf16[1,192,1152]{2,1,0:T(8,128)(2,1)}, bf16[1,192,1152]{2,1,0:T(8,128)(2,1)S(1)}, u32[]{:S(2)}, u32[]{:S(2)}) collective-permute-start(bf16[1,192,1152]{2,1,0:T(8,128)(2,1)} %collective-permute-done.1.rest_1_), channel_id=1, source_target_pairs={{0,4},{4,0},{8,12},{12,8},{16,20},{20,16},{24,28},{28,24},{1,5},{5... | collective-permute-start | bytes 1327112 | tf_op jit(solution)/shard_map/ppermute | solution.py:356
  84.9 15.1 %collective-permute-start.7 = (bf16[1,192,1152]{2,1,0:T(8,128)(2,1)}, bf16[1,192,1152]{2,1,0:T(8,128)(2,1)S(1)}, u32[]{:S(2)}, u32[]{:S(2)}) collective-permute-start(bf16[1,192,1152]{2,1,0:T(8,128)(2,1)} %collective-permute-done.2.rest_2_), channel_id=1, source_target_pairs={{0,4},{4,0},{8,12},{12,8},{16,20},{20,16},{24,28},{28,24},{1,5},{5... | collective-permute-start | bytes 1327112 | tf_op jit(solution)/shard_map/ppermute | solution.py:356
  94.3 7.1 %copy-start.5 = (bf16[1,192,1152]{2,1,0:T(8,128)(2,1)}, bf16[1,192,1152]{2,1,0:T(8,128)(2,1)S(1)}, u32[]{:S(2)}) copy-start(bf16[1,192,1152]{2,1,0:T(8,128)(2,1)S(1)} %collective-permute-done.6.rest_6_) | copy-start | bytes 1327108
  94.3 16.1 %collective-permute-start.8 = (bf16[1,192,1152]{2,1,0:T(8,128)(2,1)}, bf16[1,192,1152]{2,1,0:T(8,128)(2,1)}, u32[]{:S(2)}, u32[]{:S(2)}) collective-permute-start(bf16[1,192,1152]{2,1,0:T(8,128)(2,1)} %collective-permute-done.1.rest_1_), channel_id=1, source_target_pairs={{0,8},{4,12},{8,16},{12,20},{16,24},{20,28},{1,9},{5,13},{9,17},{1... | collective-permute-start | bytes 1327112 | tf_op jit(solution)/shard_map/ppermute | solution.py:357
  100.0 1.3 copy-start.6
  100.0 10.7 %collective-permute-start.9 = (bf16[1,192,1152]{2,1,0:T(8,128)(2,1)}, bf16[1,192,1152]{2,1,0:T(8,128)(2,1)}, u32[]{:S(2)}, u32[]{:S(2)}) collective-permute-start(bf16[1,192,1152]{2,1,0:T(8,128)(2,1)} %collective-permute-done.2.rest_2_), channel_id=1, source_target_pairs={{8,0},{12,4},{16,8},{20,12},{24,16},{28,20},{9,1},{13,5},{17,9},{2... | collective-permute-start | bytes 1327112 | tf_op jit(solution)/shard_map/ppermute | solution.py:357
Sparse Core Ops, SparseCore 0:
  51.6 14.4 all-gather.2

commit v3 on v2

--- a/solution.py
+++ b/solution.py
@@ -33,7 +33,7 @@
 
 LINE = 4
 MASKED = -1e30
-N_EARLY = 10
+N_EARLY = 9
 
 
 def layer_kernel(
@@ -136,14 +136,14 @@
 
             @pl.when((origin >= 0) & (origin < LINE))
             def _():
-                if not (finish or (early and (dist == 1 or (w == 0 and dist == 2)))):
+                if not (finish or (early and dist == 1)):
                     z_copy(w, origin, za, 0).wait_recv()
                 z_send(w, origin, (-side,), finish)
                 y_send(w, origin, yb, (-1, 1), finish)
 
     def y_wait(w, a):
         if early:
-            @pl.when(jnp.abs(a - za) > (1 if w == 0 else 0))
+            @pl.when(a != za)
             def _():
                 y_copy(w, a, 1 - yb, yb, 0).wait_recv()
             return
@@ -163,8 +163,8 @@
         def _():
             copy.wait()
     if early:
+        relay(0, 1)
         relay(1, 1)
-        relay(0, 2)
     else:
         own(0)
         own(1)
@@ -193,6 +193,7 @@
     heads(0, third)
     if early:
         relay(2, 1)
+        relay(0, 2)
     else:
         relay(0, 1)
         relay(1, 1)
@@ -316,7 +317,7 @@
     for w in range(3):
         if not early:
             own(w, True)
-        for dist in range(2 if early and w == 0 else 1, LINE):
+        for dist in range(1, LINE):
             relay(w, dist, True)
     if not early:
         @pl.loop(0, 3)
@@ -333,8 +334,7 @@
 
 
 EARLY_BLOCKS = [
-    (0, 0, 1), (0, -1, 0), (0, 1, 0), (1, 0, 1), (1, -1, 0), (1, 1, 0),
-    (0, -1, 1), (0, 1, 1), (0, -2, 0), (0, 2, 0),
+    (w, step, other) for w in range(3) for step, other in ((0, 1), (-1, 0), (1, 0))
 ]
 
 
@@ -347,14 +347,10 @@
     ahead = [(r, r + cross) for r in range(requests - cross)]
     back = [(r + cross, r) for r in range(requests - cross)]
     send = functools.partial(lax.ppermute, axis_name="req")
-    gate = w_gate[None]
-    pair = jnp.stack([w_up, w_down])
-    gate_low, gate_high = send(gate, perm=ahead), send(gate, perm=back)
     return [
-        send(gate, perm=swap), gate_low, gate_high,
-        send(pair, perm=swap), send(pair, perm=ahead), send(pair, perm=back),
-        send(gate_low, perm=swap), send(gate_high, perm=swap),
-        send(gate_low, perm=ahead), send(gate_high, perm=back),
+        send(shard[None], perm=perm)
+        for shard in (w_gate, w_up, w_down)
+        for perm in (swap, ahead, back)
     ]
 
 

time: 240 us -> 227 us (0.946)
  waiting for transfers between devices: 36.9 us -> 19.5 us
  Pallas kernels: 118 us -> 127 us
  local copies, waits for them, and re-layouts: 23.3 us -> 20 us
  starting transfers between devices: 24.6 us -> 27.8 us
  other arithmetic: 8.34 us -> 5.17 us
    ppermute x10 -> x9, waiting for transfers between devices: 27.3 us -> 2.98 us  [early_blocks(): send(shard[None], perm=perm)]
    pallas_call x1, Pallas kernels: 118 us -> 127 us  [fused_layer(): pl.pallas_call(functools.partial(layer_kernel, (n_req, n_mlp, int(len(ear...]
    all_to_all x1, waiting for transfers between devices: 9.61 us -> 16.5 us  [body(): lax.all_to_all(outgoing, 'req', split_axis=0, concat_axis=0, tiled=True)]
    ppermute x10 -> x9, starting transfers between devices: 17.2 us -> 20.4 us  [early_blocks(): send(shard[None], perm=perm)]
  transfers between devices with their start and end apart: 12 -> 11, of which waited for: 5 -> 2; matrix products, arithmetic and copies ran while one was open for 12% -> 9% of each run, Pallas kernels for 0% -> 0%
where the time goes in v3:
time: 227 us
  Pallas kernels  127 us (56%)
  starting transfers between devices  27.8 us (12%)
  between operations  21.5 us (9%)
  local copies, waits for them, and re-layouts  20 us (9%)
  waiting for transfers between devices  19.5 us (9%)
  matrix products  5.72 us (3%)
  other arithmetic  5.17 us (2%)
    pallas_call x1, Pallas kernels, fused_layer(): pl.pallas_call(functools.partial(layer_kernel, (n_req, n_mlp, int(len(ear...  127 us
    ppermute x9, starting transfers between devices, early_blocks(): send(shard[None], perm=perm)  20.4 us
    all_to_all x1, waiting for transfers between devices, body(): lax.all_to_all(outgoing, 'req', split_axis=0, concat_axis=0, tiled=True)  16.5 us
    all_to_all x1, starting transfers between devices, body(): lax.all_to_all(outgoing, 'req', split_axis=0, concat_axis=0, tiled=True)  7.43 us
  transfers between devices with their start and end apart: 11, of which 2 were waited for; matrix products, arithmetic and copies ran while one was open for 9% of the time, Pallas kernels for 0%

profile of v3, /device:TPU:0, one launch (start us, length us, event | category | flops | bytes accessed | tf_op | source)
XLA Modules:
  0.0 226.5 jit_solution(5692327218629991866)
XLA Ops:
  6.5 0.7 compare_select_fusion
  7.3 1.3 gather_fusion
  8.6 0.7 and_select_fusion.1
  9.3 0.7 fusion.26
  9.9 1.3 constant_dynamic-slice_fusion.1
  11.3 0.8 fusion.4
  12.0 1.2 copy.26
  13.3 7.4 %all-to-all-start = ((bf16[8,2,128,256]{3,2,1,0:T(8,128)(2,1)}), bf16[8,2,128,256]{3,2,1,0:T(8,128)(2,1)S(1)}, u32[]{:S(2)}, u32[]{:S(2)}) async-start(bf16[8,2,128,256]{3,2,1,0:T(8,128)(2,1)} %copy.26), calls=%async_computation | async-start | bytes 2097152 | tf_op jit(solution)/shard_map/all_to_all | solution.py:434
  26.8 0.7 constant_dynamic-slice_fusion.3
  29.9 16.5 %all-to-all-done = bf16[8,2,128,256]{3,2,1,0:T(8,128)(2,1)S(1)} async-done(((bf16[8,2,128,256]{3,2,1,0:T(8,128)(2,1)}), bf16[8,2,128,256]{3,2,1,0:T(8,128)(2,1)S(1)}, u32[]{:S(2)}, u32[]{:S(2)}) %all-to-all-start) | async-done | bytes 1048608 | tf_op jit(solution)/shard_map/all_to_all | solution.py:434
  46.9 0.7 maximum_maximum_fusion
  47.6 1.5 collective-permute-start
  49.1 2.1 collective-permute-start.1
  51.2 1.3 collective-permute-start.2
  52.5 0.9 collective-permute-start.3
  53.4 5.3 %collective-permute-start.4 = (bf16[1,192,1152]{2,1,0:T(8,128)(2,1)}, bf16[1,192,1152]{2,1,0:T(8,128)(2,1)}, u32[]{:S(2)}, u32[]{:S(2)}) collective-permute-start(bf16[1,192,1152]{2,1,0:T(8,128)(2,1)} %bitcast.24), channel_id=1, source_target_pairs={{0,8},{4,12},{8,16},{12,20},{16,24},{20,28},{1,9},{5,13},{9,17},{1... | collective-permute-start | bytes 1327112 | tf_op jit(solution)/shard_map/ppermute | solution.py:351
  60.9 4.4 %fusion.8 = f32[256,1536]{0,1:T(8,128)S(1)} fusion(bf16[1536,1536]{1,0:T(8,128)(2,1)} %param.16, bf16[256,1536]{1,0:T(8,128)(2,1)S(1)} %copy-done.2, f32[1536]{0:T(1024)S(1)} %copy-done.7, f32[256]{0:T(256)S(1)} %add_rsqrt_fusion), kind=kOutput, calls=%fused_computation.16 | convolution fusion | flops 1209532416 | bytes 7085056 | tf_op jit(solution)/shard_map/dot_general | solution.py:442
  65.7 1.2 copy.29.q_ref
  66.9 0.6 broadcast_in_dim.14.gain_ref
  67.5 0.6 compare_convert_fusion.ok_ref
  68.1 1.5 copy.39
  69.6 1.3 collective-permute-start.5
  70.9 1.2 collective-permute-start.6
  72.2 5.3 %collective-permute-start.7 = (bf16[1,192,1152]{2,1,0:T(8,128)(2,1)}, bf16[1,192,1152]{2,1,0:T(8,128)(2,1)}, u32[]{:S(2)}, u32[]{:S(2)}) collective-permute-start(bf16[1,192,1152]{2,1,0:T(8,128)(2,1)} %bitcast.25), channel_id=1, source_target_pairs={{0,8},{4,12},{8,16},{12,20},{16,24},{20,28},{1,9},{5,13},{9,17},{1... | collective-permute-start | bytes 1327112 | tf_op jit(solution)/shard_map/ppermute | solution.py:351
  77.5 1.5 collective-permute-start.8
  79.1 1.9 dynamic_update_slice.13
  81.0 2.7 %dynamic_update_slice.14 = bf16[3584,256]{1,0:T(8,128)(2,1)S(1)} dynamic-update-slice(bf16[3584,256]{1,0:T(8,128)(2,1)S(1)} %dynamic_update_slice.13, bf16[512,256]{1,0:T(8,128)(2,1)} %bitcast.51, s32[]{:T(128)S(6)} %select_n.68, s32[]{:T(128)} %constant.64.clone.1) | dynamic-update-slice | bytes 524292 | tf_op jit(solution)/shard_map/dynamic_update_slice | solution.py:459
  83.7 3.0 %dynamic_update_slice.15 = bf16[3584,256]{1,0:T(8,128)(2,1)S(1)} dynamic-update-slice(bf16[3584,256]{1,0:T(8,128)(2,1)S(1)} %dynamic_update_slice.14, bf16[1024,256]{1,0:T(8,128)(2,1)S(1)} %bitcast.43, s32[]{:T(128)S(6)} %select_n.69, s32[]{:T(128)} %constant.64.clone.1) | dynamic-update-slice | bytes 1048580 | tf_op jit(solution)/shard_map/dynamic_update_slice | solution.py:460
  86.8 1.0 constant_dynamic-slice_fusion.kv_ref
  87.8 3.0 %collective-permute-done.8.rest_8_ = bf16[1,192,1152]{2,1,0:T(8,128)(2,1)} collective-permute-done((bf16[1,192,1152]{2,1,0:T(8,128)(2,1)}, bf16[1,192,1152]{2,1,0:T(8,128)(2,1)}, u32[]{:S(2)}, u32[]{:S(2)}) %collective-permute-start.8) | collective-permute-done | bytes 442400 | tf_op jit(solution)/shard_map/ppermute | solution.py:351
  90.8 126.8 %shard_map.136 = bf16[256,1536]{1,0:T(8,128)(2,1)} custom-call(bf16[256,1536]{1,0:T(8,128)(2,1)} %copy.29.q_ref, bf16[1280,256]{1,0:T(8,128)(2,1)} %constant_dynamic-slice_fusion.kv_ref, s32[1,1280]{1,0:T(1,128)} %compare_convert_fusion.ok_ref, bf16[256,1536]{1,0:T(8,128)(2,1)} %tok_ref.1, f32[1,1536]{1,0:T(1,128)} %broadcast_in_dim.14.gain_ref, ...), custom_call_target="tpu_custom_call" | custom-call | tf_op jit(solution)/shard_map/pallas_call | solution.py:366
  217.6 2.1 copy.48
  (50 shorter events, 4.0 us)
Async XLA Ops:
  6.5 18.9 %copy-start = (bf16[1536,256]{1,0:T(8,128)(2,1)S(1)}, bf16[1536,256]{1,0:T(8,128)(2,1)}, u32[]{:S(2)}) copy-start(bf16[1536,256]{1,0:T(8,128)(2,1)} %param.17) | copy-start | bytes 2359300
  13.2 7.5 %copy-start.5 = (s32[8]{0:T(128)S(1)}, s32[8]{0:T(128)}, u32[]{:S(2)}) copy-start(s32[8]{0:T(128)} %param.25) | copy-start | bytes 100
  13.2 10.0 %copy-start.1 = (s32[64]{0:T(128)S(1)}, s32[64]{0:T(128)}, u32[]{:S(2)}) copy-start(s32[64]{0:T(128)} %param.26) | copy-start | bytes 772
  13.3 11.9 %copy-start.2 = (bf16[256,1536]{1,0:T(8,128)(2,1)S(1)}, bf16[256,1536]{1,0:T(8,128)(2,1)}, u32[]{:S(2)}) copy-start(bf16[256,1536]{1,0:T(8,128)(2,1)} %tok_ref.1) | copy-start | bytes 2359300
  13.3 12.2 %copy-start.7 = (f32[1536]{0:T(1024)S(1)}, f32[1536]{0:T(1024)}, u32[]{:S(2)}) copy-start(f32[1536]{0:T(1024)} %param.15) | copy-start | bytes 18436
  13.3 33.2 %all-to-all-start = ((bf16[8,2,128,256]{3,2,1,0:T(8,128)(2,1)}), bf16[8,2,128,256]{3,2,1,0:T(8,128)(2,1)S(1)}, u32[]{:S(2)}, u32[]{:S(2)}) async-start(bf16[8,2,128,256]{3,2,1,0:T(8,128)(2,1)} %copy.26), calls=%async_computation | async-start | bytes 2097152 | tf_op jit(solution)/shard_map/all_to_all | solution.py:434
  20.7 6.1 %copy-start.6 = (s32[3,64]{1,0:T(4,128)S(1)}, s32[3,64]{1,0:T(4,128)}, u32[]{:S(2)}) copy-start(s32[3,64]{1,0:T(4,128)} %param.27) | copy-start | bytes 2308
  20.7 47.4 %all-gather.3.cloned.1.call-start = ((), (), s32[]{:S(2)}) async-start(), calls=%async_computation.1 | async-start | bytes 1310720 | tf_op jit(solution)/shard_map/all_gather | solution.py:450
  26.0 21.6 %copy-start.3 = (bf16[192,1152]{1,0:T(8,128)(2,1)S(1)}, bf16[192,1152]{1,0:T(8,128)(2,1)}, u32[]{:S(2)}) copy-start(bf16[192,1152]{1,0:T(8,128)(2,1)} %wg_hbm.1) | copy-start | bytes 1327108
  47.6 22.0 %collective-permute-start = (bf16[1,192,1152]{2,1,0:T(8,128)(2,1)S(1)}, bf16[1,192,1152]{2,1,0:T(8,128)(2,1)}, u32[]{:S(2)}, u32[]{:S(2)}) collective-permute-start(bf16[1,192,1152]{2,1,0:T(8,128)(2,1)S(1)} %bitcast.48), channel_id=1, source_target_pairs={{0,4},{4,0},{8,12},{12,8},{16,20},{20,16},{24,28},{28,24},{1,5},{5... | collective-permute-start | bytes 1327112 | tf_op jit(solution)/shard_map/ppermute | solution.py:351
  49.1 21.8 %collective-permute-start.1 = (bf16[1,192,1152]{2,1,0:T(8,128)(2,1)S(1)}, bf16[1,192,1152]{2,1,0:T(8,128)(2,1)}, u32[]{:S(2)}, u32[]{:S(2)}) collective-permute-start(bf16[1,192,1152]{2,1,0:T(8,128)(2,1)S(1)} %bitcast.49), channel_id=1, source_target_pairs={{0,8},{4,12},{8,16},{12,20},{16,24},{20,28},{1,9},{5,13},{9,17},{1... | collective-permute-start | bytes 1327112 | tf_op jit(solution)/shard_map/ppermute | solution.py:351
  51.2 21.0 %collective-permute-start.2 = (bf16[1,192,1152]{2,1,0:T(8,128)(2,1)S(1)}, bf16[1,192,1152]{2,1,0:T(8,128)(2,1)}, u32[]{:S(2)}, u32[]{:S(2)}) collective-permute-start(bf16[1,192,1152]{2,1,0:T(8,128)(2,1)S(1)} %bitcast.50), channel_id=1, source_target_pairs={{8,0},{12,4},{16,8},{20,12},{24,16},{28,20},{9,1},{13,5},{17,9},{2... | collective-permute-start | bytes 1327112 | tf_op jit(solution)/shard_map/ppermute | solution.py:351
  52.5 25.0 %collective-permute-start.3 = (bf16[1,192,1152]{2,1,0:T(8,128)(2,1)}, bf16[1,192,1152]{2,1,0:T(8,128)(2,1)}, u32[]{:S(2)}, u32[]{:S(2)}) collective-permute-start(bf16[1,192,1152]{2,1,0:T(8,128)(2,1)} %bitcast.24), channel_id=1, source_target_pairs={{0,4},{4,0},{8,12},{12,8},{16,20},{20,16},{24,28},{28,24},{1,5},{5... | collective-permute-start | bytes 1327112 | tf_op jit(solution)/shard_map/ppermute | solution.py:351
  53.4 34.4 %collective-permute-start.4 = (bf16[1,192,1152]{2,1,0:T(8,128)(2,1)}, bf16[1,192,1152]{2,1,0:T(8,128)(2,1)}, u32[]{:S(2)}, u32[]{:S(2)}) collective-permute-start(bf16[1,192,1152]{2,1,0:T(8,128)(2,1)} %bitcast.24), channel_id=1, source_target_pairs={{0,8},{4,12},{8,16},{12,20},{16,24},{20,28},{1,9},{5,13},{9,17},{1... | collective-permute-start | bytes 1327112 | tf_op jit(solution)/shard_map/ppermute | solution.py:351
  65.5 1.4 copy-start.4
  69.6 18.2 %collective-permute-start.5 = (bf16[1,192,1152]{2,1,0:T(8,128)(2,1)}, bf16[1,192,1152]{2,1,0:T(8,128)(2,1)}, u32[]{:S(2)}, u32[]{:S(2)}) collective-permute-start(bf16[1,192,1152]{2,1,0:T(8,128)(2,1)} %bitcast.24), channel_id=1, source_target_pairs={{8,0},{12,4},{16,8},{20,12},{24,16},{28,20},{9,1},{13,5},{17,9},{2... | collective-permute-start | bytes 1327112 | tf_op jit(solution)/shard_map/ppermute | solution.py:351
  70.9 16.9 %collective-permute-start.6 = (bf16[1,192,1152]{2,1,0:T(8,128)(2,1)}, bf16[1,192,1152]{2,1,0:T(8,128)(2,1)}, u32[]{:S(2)}, u32[]{:S(2)}) collective-permute-start(bf16[1,192,1152]{2,1,0:T(8,128)(2,1)} %bitcast.25), channel_id=1, source_target_pairs={{0,4},{4,0},{8,12},{12,8},{16,20},{20,16},{24,28},{28,24},{1,5},{5... | collective-permute-start | bytes 1327112 | tf_op jit(solution)/shard_map/ppermute | solution.py:351
  72.2 15.7 %collective-permute-start.7 = (bf16[1,192,1152]{2,1,0:T(8,128)(2,1)}, bf16[1,192,1152]{2,1,0:T(8,128)(2,1)}, u32[]{:S(2)}, u32[]{:S(2)}) collective-permute-start(bf16[1,192,1152]{2,1,0:T(8,128)(2,1)} %bitcast.25), channel_id=1, source_target_pairs={{0,8},{4,12},{8,16},{12,20},{16,24},{20,28},{1,9},{5,13},{9,17},{1... | collective-permute-start | bytes 1327112 | tf_op jit(solution)/shard_map/ppermute | solution.py:351
  77.5 13.3 %collective-permute-start.8 = (bf16[1,192,1152]{2,1,0:T(8,128)(2,1)}, bf16[1,192,1152]{2,1,0:T(8,128)(2,1)}, u32[]{:S(2)}, u32[]{:S(2)}) collective-permute-start(bf16[1,192,1152]{2,1,0:T(8,128)(2,1)} %bitcast.25), channel_id=1, source_target_pairs={{8,0},{12,4},{16,8},{20,12},{24,16},{28,20},{9,1},{13,5},{17,9},{2... | collective-permute-start | bytes 1327112 | tf_op jit(solution)/shard_map/ppermute | solution.py:351
Sparse Core Ops, SparseCore 0:
  47.7 15.7 all-gather.2

commit v4 on v3

--- a/solution.py
+++ b/solution.py
@@ -204,7 +204,8 @@
         own(2)
         relay(0, 2)
     heads(2 * third, HEADS - 2 * third)
-    relay(0, 3) if early else relay(1, 2)
+    if not early:
+        relay(1, 2)
     loads[3].wait()
 
     @pl.loop(0, LINE)
@@ -231,7 +232,7 @@
         t_copy(mine, toward, ts.at[toward]).start()
     if early:
         relay(2, 2)
-        relay(1, 3)
+        relay(0, 3)
     else:
         relay(2, 1)
         relay(0, 3)
@@ -240,6 +241,8 @@
     for owner in alike:
         t_copy(owner, mine, ts.at[0]).wait_recv()
         t_copy(owner, sibling, tf.at[owner]).start()
+    if early:
+        relay(1, 3)
     for w in range(2):
         for a in range(LINE):
             y_wait(w, a)

time: 227 us -> 227 us (level)
  no operation moved by 1% of the time
where the time goes in v4:
time: 227 us
  Pallas kernels  127 us (56%)
  starting transfers between devices  27.8 us (12%)
  between operations  21.5 us (9%)
  local copies, waits for them, and re-layouts  20 us (9%)
  waiting for transfers between devices  19.5 us (9%)
  matrix products  5.72 us (3%)
  other arithmetic  5.17 us (2%)
    pallas_call x1, Pallas kernels, fused_layer(): pl.pallas_call(functools.partial(layer_kernel, (n_req, n_mlp, int(len(ear...  127 us
    ppermute x9, starting transfers between devices, early_blocks(): send(shard[None], perm=perm)  20.4 us
    all_to_all x1, waiting for transfers between devices, body(): lax.all_to_all(outgoing, 'req', split_axis=0, concat_axis=0, tiled=True)  16.5 us
    all_to_all x1, starting transfers between devices, body(): lax.all_to_all(outgoing, 'req', split_axis=0, concat_axis=0, tiled=True)  7.43 us
  transfers between devices with their start and end apart: 11, of which 2 were waited for; matrix products, arithmetic and copies ran while one was open for 9% of the time, Pallas kernels for 0%

profile of v4, /device:TPU:0, one launch (start us, length us, event | category | flops | bytes accessed | tf_op | source)
XLA Modules:
  0.0 226.5 jit_solution(16041035920063666704)
XLA Ops:
  6.5 0.7 compare_select_fusion
  7.3 1.3 gather_fusion
  8.6 0.7 and_select_fusion.1
  9.3 0.7 fusion.26
  9.9 1.3 constant_dynamic-slice_fusion.1
  11.3 0.8 fusion.4
  12.0 1.2 copy.26
  13.3 7.4 %all-to-all-start = ((bf16[8,2,128,256]{3,2,1,0:T(8,128)(2,1)}), bf16[8,2,128,256]{3,2,1,0:T(8,128)(2,1)S(1)}, u32[]{:S(2)}, u32[]{:S(2)}) async-start(bf16[8,2,128,256]{3,2,1,0:T(8,128)(2,1)} %copy.26), calls=%async_computation | async-start | bytes 2097152 | tf_op jit(solution)/shard_map/all_to_all | solution.py:437
  26.8 0.7 constant_dynamic-slice_fusion.3
  29.9 16.5 %all-to-all-done = bf16[8,2,128,256]{3,2,1,0:T(8,128)(2,1)S(1)} async-done(((bf16[8,2,128,256]{3,2,1,0:T(8,128)(2,1)}), bf16[8,2,128,256]{3,2,1,0:T(8,128)(2,1)S(1)}, u32[]{:S(2)}, u32[]{:S(2)}) %all-to-all-start) | async-done | bytes 1048608 | tf_op jit(solution)/shard_map/all_to_all | solution.py:437
  46.9 0.7 maximum_maximum_fusion
  47.6 1.5 collective-permute-start
  49.1 2.1 collective-permute-start.1
  51.2 1.3 collective-permute-start.2
  52.5 0.9 collective-permute-start.3
  53.4 5.3 %collective-permute-start.4 = (bf16[1,192,1152]{2,1,0:T(8,128)(2,1)}, bf16[1,192,1152]{2,1,0:T(8,128)(2,1)}, u32[]{:S(2)}, u32[]{:S(2)}) collective-permute-start(bf16[1,192,1152]{2,1,0:T(8,128)(2,1)} %bitcast.24), channel_id=1, source_target_pairs={{0,8},{4,12},{8,16},{12,20},{16,24},{20,28},{1,9},{5,13},{9,17},{1... | collective-permute-start | bytes 1327112 | tf_op jit(solution)/shard_map/ppermute | solution.py:354
  60.9 4.4 %fusion.8 = f32[256,1536]{0,1:T(8,128)S(1)} fusion(bf16[1536,1536]{1,0:T(8,128)(2,1)} %param.16, bf16[256,1536]{1,0:T(8,128)(2,1)S(1)} %copy-done.2, f32[1536]{0:T(1024)S(1)} %copy-done.7, f32[256]{0:T(256)S(1)} %add_rsqrt_fusion), kind=kOutput, calls=%fused_computation.16 | convolution fusion | flops 1209532416 | bytes 7085056 | tf_op jit(solution)/shard_map/dot_general | solution.py:445
  65.7 1.2 copy.29.q_ref
  66.9 0.6 broadcast_in_dim.14.gain_ref
  67.5 0.6 compare_convert_fusion.ok_ref
  68.1 1.5 copy.39
  69.6 1.3 collective-permute-start.5
  70.9 1.2 collective-permute-start.6
  72.2 5.3 %collective-permute-start.7 = (bf16[1,192,1152]{2,1,0:T(8,128)(2,1)}, bf16[1,192,1152]{2,1,0:T(8,128)(2,1)}, u32[]{:S(2)}, u32[]{:S(2)}) collective-permute-start(bf16[1,192,1152]{2,1,0:T(8,128)(2,1)} %bitcast.25), channel_id=1, source_target_pairs={{0,8},{4,12},{8,16},{12,20},{16,24},{20,28},{1,9},{5,13},{9,17},{1... | collective-permute-start | bytes 1327112 | tf_op jit(solution)/shard_map/ppermute | solution.py:354
  77.5 1.5 collective-permute-start.8
  79.1 1.9 dynamic_update_slice.13
  81.0 2.7 %dynamic_update_slice.14 = bf16[3584,256]{1,0:T(8,128)(2,1)S(1)} dynamic-update-slice(bf16[3584,256]{1,0:T(8,128)(2,1)S(1)} %dynamic_update_slice.13, bf16[512,256]{1,0:T(8,128)(2,1)} %bitcast.51, s32[]{:T(128)S(6)} %select_n.68, s32[]{:T(128)} %constant.64.clone.1) | dynamic-update-slice | bytes 524292 | tf_op jit(solution)/shard_map/dynamic_update_slice | solution.py:462
  83.7 3.0 %dynamic_update_slice.15 = bf16[3584,256]{1,0:T(8,128)(2,1)S(1)} dynamic-update-slice(bf16[3584,256]{1,0:T(8,128)(2,1)S(1)} %dynamic_update_slice.14, bf16[1024,256]{1,0:T(8,128)(2,1)S(1)} %bitcast.43, s32[]{:T(128)S(6)} %select_n.69, s32[]{:T(128)} %constant.64.clone.1) | dynamic-update-slice | bytes 1048580 | tf_op jit(solution)/shard_map/dynamic_update_slice | solution.py:463
  86.8 1.0 constant_dynamic-slice_fusion.kv_ref
  87.8 3.0 %collective-permute-done.8.rest_8_ = bf16[1,192,1152]{2,1,0:T(8,128)(2,1)} collective-permute-done((bf16[1,192,1152]{2,1,0:T(8,128)(2,1)}, bf16[1,192,1152]{2,1,0:T(8,128)(2,1)}, u32[]{:S(2)}, u32[]{:S(2)}) %collective-permute-start.8) | collective-permute-done | bytes 442400 | tf_op jit(solution)/shard_map/ppermute | solution.py:354
  90.8 126.8 %shard_map.136 = bf16[256,1536]{1,0:T(8,128)(2,1)} custom-call(bf16[256,1536]{1,0:T(8,128)(2,1)} %copy.29.q_ref, bf16[1280,256]{1,0:T(8,128)(2,1)} %constant_dynamic-slice_fusion.kv_ref, s32[1,1280]{1,0:T(1,128)} %compare_convert_fusion.ok_ref, bf16[256,1536]{1,0:T(8,128)(2,1)} %tok_ref.1, f32[1,1536]{1,0:T(1,128)} %broadcast_in_dim.14.gain_ref, ...), custom_call_target="tpu_custom_call" | custom-call | tf_op jit(solution)/shard_map/pallas_call | solution.py:369
  217.6 2.1 copy.48
  (50 shorter events, 4.0 us)
Async XLA Ops:
  6.5 18.9 %copy-start = (bf16[1536,256]{1,0:T(8,128)(2,1)S(1)}, bf16[1536,256]{1,0:T(8,128)(2,1)}, u32[]{:S(2)}) copy-start(bf16[1536,256]{1,0:T(8,128)(2,1)} %param.17) | copy-start | bytes 2359300
  13.2 7.5 %copy-start.5 = (s32[8]{0:T(128)S(1)}, s32[8]{0:T(128)}, u32[]{:S(2)}) copy-start(s32[8]{0:T(128)} %param.25) | copy-start | bytes 100
  13.2 10.0 %copy-start.1 = (s32[64]{0:T(128)S(1)}, s32[64]{0:T(128)}, u32[]{:S(2)}) copy-start(s32[64]{0:T(128)} %param.26) | copy-start | bytes 772
  13.3 11.9 %copy-start.2 = (bf16[256,1536]{1,0:T(8,128)(2,1)S(1)}, bf16[256,1536]{1,0:T(8,128)(2,1)}, u32[]{:S(2)}) copy-start(bf16[256,1536]{1,0:T(8,128)(2,1)} %tok_ref.1) | copy-start | bytes 2359300
  13.3 12.2 %copy-start.7 = (f32[1536]{0:T(1024)S(1)}, f32[1536]{0:T(1024)}, u32[]{:S(2)}) copy-start(f32[1536]{0:T(1024)} %param.15) | copy-start | bytes 18436
  13.3 33.2 %all-to-all-start = ((bf16[8,2,128,256]{3,2,1,0:T(8,128)(2,1)}), bf16[8,2,128,256]{3,2,1,0:T(8,128)(2,1)S(1)}, u32[]{:S(2)}, u32[]{:S(2)}) async-start(bf16[8,2,128,256]{3,2,1,0:T(8,128)(2,1)} %copy.26), calls=%async_computation | async-start | bytes 2097152 | tf_op jit(solution)/shard_map/all_to_all | solution.py:437
  20.7 6.1 %copy-start.6 = (s32[3,64]{1,0:T(4,128)S(1)}, s32[3,64]{1,0:T(4,128)}, u32[]{:S(2)}) copy-start(s32[3,64]{1,0:T(4,128)} %param.27) | copy-start | bytes 2308
  20.7 47.4 %all-gather.3.cloned.1.call-start = ((), (), s32[]{:S(2)}) async-start(), calls=%async_computation.1 | async-start | bytes 1310720 | tf_op jit(solution)/shard_map/all_gather | solution.py:453
  26.0 21.6 %copy-start.3 = (bf16[192,1152]{1,0:T(8,128)(2,1)S(1)}, bf16[192,1152]{1,0:T(8,128)(2,1)}, u32[]{:S(2)}) copy-start(bf16[192,1152]{1,0:T(8,128)(2,1)} %wg_hbm.1) | copy-start | bytes 1327108
  47.6 22.0 %collective-permute-start = (bf16[1,192,1152]{2,1,0:T(8,128)(2,1)S(1)}, bf16[1,192,1152]{2,1,0:T(8,128)(2,1)}, u32[]{:S(2)}, u32[]{:S(2)}) collective-permute-start(bf16[1,192,1152]{2,1,0:T(8,128)(2,1)S(1)} %bitcast.48), channel_id=1, source_target_pairs={{0,4},{4,0},{8,12},{12,8},{16,20},{20,16},{24,28},{28,24},{1,5},{5... | collective-permute-start | bytes 1327112 | tf_op jit(solution)/shard_map/ppermute | solution.py:354
  49.1 21.8 %collective-permute-start.1 = (bf16[1,192,1152]{2,1,0:T(8,128)(2,1)S(1)}, bf16[1,192,1152]{2,1,0:T(8,128)(2,1)}, u32[]{:S(2)}, u32[]{:S(2)}) collective-permute-start(bf16[1,192,1152]{2,1,0:T(8,128)(2,1)S(1)} %bitcast.49), channel_id=1, source_target_pairs={{0,8},{4,12},{8,16},{12,20},{16,24},{20,28},{1,9},{5,13},{9,17},{1... | collective-permute-start | bytes 1327112 | tf_op jit(solution)/shard_map/ppermute | solution.py:354
  51.2 21.0 %collective-permute-start.2 = (bf16[1,192,1152]{2,1,0:T(8,128)(2,1)S(1)}, bf16[1,192,1152]{2,1,0:T(8,128)(2,1)}, u32[]{:S(2)}, u32[]{:S(2)}) collective-permute-start(bf16[1,192,1152]{2,1,0:T(8,128)(2,1)S(1)} %bitcast.50), channel_id=1, source_target_pairs={{8,0},{12,4},{16,8},{20,12},{24,16},{28,20},{9,1},{13,5},{17,9},{2... | collective-permute-start | bytes 1327112 | tf_op jit(solution)/shard_map/ppermute | solution.py:354
  52.5 25.0 %collective-permute-start.3 = (bf16[1,192,1152]{2,1,0:T(8,128)(2,1)}, bf16[1,192,1152]{2,1,0:T(8,128)(2,1)}, u32[]{:S(2)}, u32[]{:S(2)}) collective-permute-start(bf16[1,192,1152]{2,1,0:T(8,128)(2,1)} %bitcast.24), channel_id=1, source_target_pairs={{0,4},{4,0},{8,12},{12,8},{16,20},{20,16},{24,28},{28,24},{1,5},{5... | collective-permute-start | bytes 1327112 | tf_op jit(solution)/shard_map/ppermute | solution.py:354
  53.4 34.4 %collective-permute-start.4 = (bf16[1,192,1152]{2,1,0:T(8,128)(2,1)}, bf16[1,192,1152]{2,1,0:T(8,128)(2,1)}, u32[]{:S(2)}, u32[]{:S(2)}) collective-permute-start(bf16[1,192,1152]{2,1,0:T(8,128)(2,1)} %bitcast.24), channel_id=1, source_target_pairs={{0,8},{4,12},{8,16},{12,20},{16,24},{20,28},{1,9},{5,13},{9,17},{1... | collective-permute-start | bytes 1327112 | tf_op jit(solution)/shard_map/ppermute | solution.py:354
  65.5 1.4 copy-start.4
  69.6 18.2 %collective-permute-start.5 = (bf16[1,192,1152]{2,1,0:T(8,128)(2,1)}, bf16[1,192,1152]{2,1,0:T(8,128)(2,1)}, u32[]{:S(2)}, u32[]{:S(2)}) collective-permute-start(bf16[1,192,1152]{2,1,0:T(8,128)(2,1)} %bitcast.24), channel_id=1, source_target_pairs={{8,0},{12,4},{16,8},{20,12},{24,16},{28,20},{9,1},{13,5},{17,9},{2... | collective-permute-start | bytes 1327112 | tf_op jit(solution)/shard_map/ppermute | solution.py:354
  70.9 16.9 %collective-permute-start.6 = (bf16[1,192,1152]{2,1,0:T(8,128)(2,1)}, bf16[1,192,1152]{2,1,0:T(8,128)(2,1)}, u32[]{:S(2)}, u32[]{:S(2)}) collective-permute-start(bf16[1,192,1152]{2,1,0:T(8,128)(2,1)} %bitcast.25), channel_id=1, source_target_pairs={{0,4},{4,0},{8,12},{12,8},{16,20},{20,16},{24,28},{28,24},{1,5},{5... | collective-permute-start | bytes 1327112 | tf_op jit(solution)/shard_map/ppermute | solution.py:354
  72.2 15.7 %collective-permute-start.7 = (bf16[1,192,1152]{2,1,0:T(8,128)(2,1)}, bf16[1,192,1152]{2,1,0:T(8,128)(2,1)}, u32[]{:S(2)}, u32[]{:S(2)}) collective-permute-start(bf16[1,192,1152]{2,1,0:T(8,128)(2,1)} %bitcast.25), channel_id=1, source_target_pairs={{0,8},{4,12},{8,16},{12,20},{16,24},{20,28},{1,9},{5,13},{9,17},{1... | collective-permute-start | bytes 1327112 | tf_op jit(solution)/shard_map/ppermute | solution.py:354
  77.5 13.3 %collective-permute-start.8 = (bf16[1,192,1152]{2,1,0:T(8,128)(2,1)}, bf16[1,192,1152]{2,1,0:T(8,128)(2,1)}, u32[]{:S(2)}, u32[]{:S(2)}) collective-permute-start(bf16[1,192,1152]{2,1,0:T(8,128)(2,1)} %bitcast.25), channel_id=1, source_target_pairs={{8,0},{12,4},{16,8},{20,12},{24,16},{28,20},{9,1},{13,5},{17,9},{2... | collective-permute-start | bytes 1327112 | tf_op jit(solution)/shard_map/ppermute | solution.py:354
Sparse Core Ops, SparseCore 0:
  47.7 15.7 all-gather.2
